TPU v7x, 32 devices: a whole 2x2x4 slice. The times are simulated.
32 devices in a mesh: rep: 4 (over y, core), fsdp: 8 (over z, x).
Axes of the slice: x: 2, y: 2, z: 4, core: 2. Of those that a mesh axis runs over, the one named last changes fastest.
Arguments:
- hidden: bfloat16 [24576, 768], P(('rep', 'fsdp')), may hold values from -6 to 6
- cotangent: bfloat16 [24576, 768], P(('rep', 'fsdp')), may hold values from -6 to 6
- lengths: int32 [192], P(('rep', 'fsdp')), may hold values from 16 to 128, as said below
- bounds: int32 [192], P(('rep', 'fsdp')), may hold values from 1 to 127, as said below
- timesteps: int32 [192], P(('rep', 'fsdp')), may hold values from 0 to 1999
- weight_qkv: bfloat16 [768, 2304], P('fsdp'), may hold values from -0.21875 to 0.21875
- bias_qv: bfloat16 [1536], P('fsdp'), may hold values from -3 to 3
- weight_out: bfloat16 [768, 768], P('fsdp'), may hold values from -0.625 to 0.625
- bias_out: bfloat16 [768], P('fsdp'), may hold values from -3 to 3
- gain_mid: bfloat16 [768], P('fsdp'), may hold values from 0.099609375 to 1.8984375
- shift_mid: bfloat16 [768], P('fsdp'), may hold values from -3 to 3
- weight_up: bfloat16 [768, 3072], P('fsdp'), may hold values from -0.21875 to 0.21875
- bias_up: bfloat16 [3072], P('fsdp'), may hold values from -3 to 3
- weight_down: bfloat16 [3072, 768], P('fsdp'), may hold values from -0.109375 to 0.109375
- bias_down: bfloat16 [768], P('fsdp'), may hold values from -3 to 3
- gain_last: bfloat16 [768], P('fsdp'), may hold values from 0.099609375 to 1.8984375
- shift_last: bfloat16 [768], P('fsdp'), may hold values from -3 to 3
- weight_time: bfloat16 [768, 128], P('fsdp'), may hold values from -0.5 to 0.5
Outputs:
- activations: bfloat16 [24576, 768], P(('rep', 'fsdp'))
- grad_hidden: bfloat16 [24576, 768], P(('rep', 'fsdp'))
- grad_weight_qkv: float32 [768, 2304], P('fsdp')
- grad_bias_qv: float32 [1536], P('fsdp')
- grad_weight_out: float32 [768, 768], P('fsdp')
- grad_bias_out: float32 [768], P('fsdp')
- grad_gain_mid: float32 [768], P('fsdp')
- grad_shift_mid: float32 [768], P('fsdp')
- grad_weight_up: float32 [768, 3072], P('fsdp')
- grad_bias_up: float32 [3072], P('fsdp')
- grad_weight_down: float32 [3072, 768], P('fsdp')
- grad_bias_down: float32 [768], P('fsdp')
- grad_gain_last: float32 [768], P('fsdp')
- grad_shift_last: float32 [768], P('fsdp')
- grad_weight_time: float32 [768, 128], P('fsdp')
Inputs may be any that keep to these rules, and one draw needn't show every extreme that they name: `lengths`: the first of each device's 6 sequences (every 6-th from 0) has length 128; sequence 1 has length 16. `bounds`: each boundary is at least 1 and below its sequence's length; sequence 0 has boundary 128 - 1 and sequence 1 has boundary 1.
All inputs are finite; a program needn't handle non-finite values.
Results may differ from a plain program's by a relative error of at most 0.019.
Values may be sent and summed in bfloat16 or wider, within the bound.
No kernel may reach another device: no remote copies, remote signals or barrier semaphores. Data moves between devices by JAX's collectives and lax.ppermute only.
A program may use at most 192 MiB of HBM per device.

v0:
```python
import functools
import math

import jax
import jax.numpy as jnp
from jax import lax
from jax.experimental import pallas as pl
from jax.experimental.pallas import tpu as pltpu
from jax.sharding import PartitionSpec as P

HEADS = 12
TFREQ = 128
XS = 2
TALL = 16
WIDE = jnp.float32
HALF = jnp.bfloat16
MIB = 1024 * 1024
(BIAS_Q, BIAS_V, BIAS_OUT, GAIN_MID, SHIFT_MID, BIAS_UP, BIAS_DOWN, GAIN_LAST, SHIFT_LAST) = (0, 1, 2, 3, 4, 5, 9, 10, 11)

ANYWHERE = pl.BlockSpec(memory_space=pltpu.HBM)
SCALARS = pl.BlockSpec(memory_space=pltpu.SMEM)


def dot(left, right, axes=(1, 0)):
    return lax.dot_general(
        left, right, (((axes[0],), (axes[1],)), ((), ())), preferred_element_type=WIDE
    )


def shape(dims, dtype=HALF):
    return jax.ShapeDtypeStruct(tuple(dims), dtype)


def held(dims, dtype=HALF):
    return pltpu.VMEM(tuple(dims), dtype)


def near(*values):
    return [pltpu.with_memory_space_constraint(v, pltpu.VMEM) for v in values]


def far(*values):
    return [pltpu.with_memory_space_constraint(v, pltpu.HBM) for v in values]


def fixed(dims):
    return pl.BlockSpec(tuple(dims), lambda *_: (0,) * len(dims))


def call(
    kernel, grid, in_specs, out_specs, out_shape, scratch=(), prefetch=(), after=(), aliases=None, vmem=24, cost=1.0, token=False
):
    after = list(after)
    count, n = len(in_specs), len(after)
    if token:
        results = len(out_specs)
        out_specs = list(out_specs) + [fixed((8, 128))]
        out_shape = list(out_shape) + [shape((8, 128), WIDE)]

    def run(*refs):
        start = len(prefetch) + count
        refs = refs[:start] + refs[start + n :]
        if token:
            there = refs[start + results]
            there[...] = jnp.zeros_like(there)
            refs = refs[: start + results] + refs[start + results + 1 :]
        kernel(*refs)

    return lambda *operands: pl.pallas_call(
        run,
        grid_spec=pltpu.PrefetchScalarGridSpec(
            num_scalar_prefetch=len(prefetch),
            grid=grid,
            in_specs=in_specs + [ANYWHERE] * n,
            out_specs=out_specs,
            scratch_shapes=list(scratch),
        ),
        out_shape=out_shape,
        input_output_aliases=aliases or {},
        compiler_params=pltpu.CompilerParams(vmem_limit_bytes=vmem * MIB),
        cost_estimate=pl.CostEstimate(flops=int(cost * 4.0e9), bytes_accessed=int(cost * 4.0e6), transcendentals=0),
    )(*prefetch, *operands, *after)


def norm_parts(value):
    mean = jnp.mean(value, -1, keepdims=True)
    centered = value - mean
    inverse = lax.rsqrt(jnp.mean(centered * centered, -1, keepdims=True) + 1e-05)
    return centered * inverse, inverse


def norm_back(grad, normed, inverse):
    return inverse * (
        grad
        - jnp.mean(grad, -1, keepdims=True)
        - normed * jnp.mean(grad * normed, -1, keepdims=True)
    )


def flip(index, by):
    return 1 - index if by else index


class Gathered:
    def __init__(self, arrays, segments, dims):
        self.arrays, self.segments, self.dims = list(arrays), list(segments), tuple(dims)
        self.zs = dims[0]

    def load(self, refs, place, target, sem):
        zs, _, _, rows, columns = self.dims
        z0, x0, y0, c0 = (place[i] for i in range(4))
        wide = columns // 2
        cut = self.arrays[0].shape[0]
        for n, low, count, dz, dx, dy, dc, column in self.segments:
            z = lax.rem(z0 + (zs - dz), zs)
            while count:
                block = column // wide
                step = min(count, (block + 1) * wide - column)
                first = pl.multiple_of(flip(c0, dc) * wide + column % wide, 128)
                there = target.at[
                    z, flip(x0, dx), flip(y0, dy), pl.ds(block * cut, cut), pl.ds(first, step)
                ]
                pltpu.make_async_copy(refs[n].at[:, pl.ds(low, step)], there, sem).start()
                low, column, count = low + step, column + step, count - step
        pltpu.make_async_copy(target, target, sem).wait()


class Whole:
    def __init__(self, array):
        self.arrays, self.dims = [array], array.shape

    def load(self, refs, place, target, sem):
        copy = pltpu.make_async_copy(refs[0], target, sem)
        copy.start()
        copy.wait()


def load(copies):
    for copy in copies:
        copy.start()
    for copy in copies:
        copy.wait()


def columns_of(ref, low, high):
    value = ref[..., low:high]
    return value.reshape(-1, high - low)


def whole_specs(values):
    return [fixed(v.shape) for v in values]


def vector_map(shards):
    index = lax.broadcasted_iota(jnp.int32, (TALL * shards, 1), 0)
    shard, r = index // TALL, index % TALL
    half, quarter = shards // 2, shards // 4
    query, up = r < 2, (r >= BIAS_UP) & (r < BIAS_DOWN)
    kinds = jnp.where(query, shard // half, jnp.where(up, BIAS_UP + shard // quarter, r))
    spots = jnp.where(
        query, 2 * (shard % half) + r, jnp.where(up, 4 * (shard % quarter) + r - BIAS_UP, shard)
    )
    return kinds, spots


def selector(width, shards):
    each = width // shards
    row = lax.broadcasted_iota(jnp.int32, (width, shards * TFREQ), 0)
    column = lax.broadcasted_iota(jnp.int32, (width, shards * TFREQ), 1)
    lane = column % TFREQ
    return ((row == (column // TFREQ) * each + lane) & (lane < each)).astype(HALF)


def kind_rows(kinds, shards):
    return (kinds == lax.broadcasted_iota(jnp.int32, (TALL * shards, TALL), 1)).astype(HALF)


def table_of(pieces, width, shards):
    kinds, spots = vector_map(shards)
    wide = jnp.concatenate([jnp.where(spots == m, pieces, jnp.zeros_like(pieces)) for m in range(shards)], axis=1)
    spread = dot(wide, selector(width, shards), (1, 1)).astype(HALF)
    return dot(kind_rows(kinds, shards), spread, (0, 0))


def pieces_of(table, width, shards):
    kinds, spots = vector_map(shards)
    spread = dot(dot(kind_rows(kinds, shards), table).astype(HALF), selector(width, shards))
    out = jnp.zeros((TALL * shards, TFREQ), WIDE)
    for m in range(shards):
        out = jnp.where(spots == m, spread[:, m * TFREQ : (m + 1) * TFREQ], out)
    return out.astype(HALF)


def add_time(start_of, bounds_ref, temb, seqs, span, use):
    places = lax.broadcasted_iota(jnp.int32, (span, 1), 0)
    for s in range(seqs):
        at = slice(s * span, (s + 1) * span)
        target = jnp.where(places >= bounds_ref[s], 1.0, 0.0)
        use(at, start_of[at, :].astype(WIDE) + target * temb[s : s + 1, :])


def project(place, bounds, hidden, feats, group, known, dims, after=()):
    rows, width, seqs = dims
    span = rows // seqs
    half = 3 * width // 2
    scale = (width // HEADS) ** (-0.5)
    n = len(group.arrays)
    wide = half + TFREQ

    def kernel(place_ref, bounds_ref, hidden_ref, feats_ref, *refs):
        ins, refs = refs[:n], refs[n:]
        if known:
            time_in, vec_in = refs[:2]
            refs = refs[2:]
        start_ref, qkv_ref, vec_ref, time_ref, w_ref, sem = refs
        group.load(ins, place_ref, w_ref, sem)
        if known:
            time_ref[...], table = time_in[...], vec_in[...]
        else:
            time_ref[...] = columns_of(w_ref, half, wide)
            shards = group.zs * XS
            pieces = columns_of(w_ref, wide + half, 2 * wide).reshape(shards, width // shards, TFREQ)
            table = table_of(pieces[:, :TALL].reshape(shards * TALL, TFREQ), width, shards)
        vec_ref[...] = table
        temb = dot(feats_ref[...], time_ref[...], (1, 1))

        def use(at, start):
            start_ref[at, :] = start.astype(HALF)

        add_time(hidden_ref, bounds_ref, temb, seqs, span, use)
        start_b = start_ref[...]
        first = dot(start_b, columns_of(w_ref, 0, half))
        qkv_ref[:, :width] = ((first[:, :width] + table[BIAS_Q : BIAS_Q + 1]) * scale).astype(HALF)
        qkv_ref[:, width:half] = first[:, width:].astype(HALF)
        second = dot(start_b, columns_of(w_ref, wide, wide + half))
        rest = half - width
        qkv_ref[:, half : half + rest] = second[:, :rest].astype(HALF)
        qkv_ref[:, 2 * width :] = (second[:, rest:] + table[BIAS_V : BIAS_V + 1]).astype(HALF)

    extra = list(known) if known else []
    outs = [held((rows, width)), held((rows, 3 * width)), held((TALL, width), WIDE), held((width, TFREQ)), held(group.dims)]
    return call(
        kernel,
        (1,),
        [SCALARS, SCALARS] + whole_specs([hidden, feats]) + [ANYWHERE] * n + whole_specs(extra),
        whole_specs(outs),
        outs,
        [pltpu.SemaphoreType.DMA],
        after=after,
        cost=0.4375, vmem=6,
    )(place, bounds, hidden, feats, *far(*group.arrays), *extra)


def attend(lens, qkv, dims, after=()):
    rows, width, seqs = dims
    span = rows // seqs
    pairs = width // 128

    def kernel(lens_ref, qkv_ref, mixed_ref, stats_ref):
        lane = lax.broadcasted_iota(jnp.int32, (span, 128), 1)
        low = lane < 64

        @pl.loop(0, seqs)
        def _(s):
            at = pl.ds(pl.multiple_of(s * span, span), span)
            keep = lane < lens_ref[s]
            stats = jnp.zeros((span, 128), WIDE)
            for p in range(pairs):
                cols = lambda m: slice(m * width + p * 128, m * width + (p + 1) * 128)
                keys = pair_split(qkv_ref[at, cols(1)], low)
                values = pair_split(qkv_ref[at, cols(2)], low)
                scores = dot(qkv_ref[at, cols(0)], keys, (1, 1))
                probs = []
                for h in range(2):
                    one = jnp.where(keep, scores[:, h * span : (h + 1) * span], -1e30)
                    top = jnp.max(one, -1, keepdims=True)
                    expo = jnp.exp(one - top)
                    total = jnp.sum(expo, -1, keepdims=True)
                    probs.append((expo * (1.0 / total)).astype(HALF))
                    stats = jnp.where(lane == 2 * p + h, top + jnp.log(total), stats)
                mixed_ref[at, cols(0)] = dot(jnp.concatenate(probs, axis=1), values).astype(HALF)
            stats_ref[at, :] = stats

    outs = [held((rows, width)), held((rows, 128), WIDE)]
    return call(
        kernel,
        (1,),
        [SCALARS] + whole_specs([qkv]),
        whole_specs(outs),
        outs,
        after=after,
        cost=0.4375, vmem=4,
    )(lens, *near(qkv))


def raise_up(place, bounds, hidden, feats, time, mixed, table, group, dims, after=()):
    rows, width, seqs = dims
    span = rows // seqs
    n = len(group.arrays)
    up, out = 2 * width, width // 2
    wide = up + out

    def kernel(place_ref, bounds_ref, hidden_ref, feats_ref, time_ref, mixed_ref, vec_ref, *refs):
        ins = refs[:n]
        normed_ref, middle_ref, inverse_ref, acted_ref, slope_ref, out_ref, w_ref, branch_ref, sem = refs[n:]
        row = lambda r: vec_ref[r : r + 1, :]
        group.load(ins, place_ref, w_ref, sem)
        for h in range(2):
            out_ref[:, h * out : (h + 1) * out] = columns_of(w_ref, h * wide + up, (h + 1) * wide)
        temb = dot(feats_ref[...], time_ref[...], (1, 1))
        branch_ref[...] = dot(mixed_ref[...], out_ref[...]) + row(BIAS_OUT)

        def use(at, start):
            normed, inverse = norm_parts(start + branch_ref[at, :])
            normed_ref[at, :] = normed
            middle_ref[at, :] = (normed * row(GAIN_MID) + row(SHIFT_MID)).astype(HALF)
            inverse_ref[at, :] = jnp.broadcast_to(inverse, (span, 128))

        add_time(hidden_ref, bounds_ref, temb, seqs, span, use)
        gelu_blocks((0, 1), middle_ref, w_ref, row, acted_ref, slope_ref, width, wide)

    outs = [
        held((rows, width), WIDE),
        held((rows, width)),
        held((rows, 128), WIDE),
        held((rows, 2 * up)),
        held((rows, 2 * up)),
        held((width, width)),
        held(group.dims),
    ]
    return call(
        kernel,
        (1,),
        [SCALARS, SCALARS] + whole_specs([hidden, feats, time, mixed, table]) + [ANYWHERE] * n,
        whole_specs(outs),
        outs,
        [pltpu.VMEM((rows, width), WIDE), pltpu.SemaphoreType.DMA],
        after=after,
        cost=0.54375, vmem=10,
    )(place, bounds, hidden, feats, *near(time, mixed, table), *far(*group.arrays))


def gelu_blocks(blocks, middle_ref, w_ref, row, acted_ref, slope_ref, width, wide):
    root = math.sqrt(2 / math.pi)
    for k in blocks:
        low = (k // 2) * wide + (k % 2) * width
        cols = slice(k * width, (k + 1) * width)
        u = dot(middle_ref[...], columns_of(w_ref, low, low + width)) + row(BIAS_UP + k)
        square = u * u
        gate = 0.5 + 0.5 * jnp.tanh(u * (root + (root * 0.044715) * square))
        acted = u * gate
        acted_ref[:, cols] = acted.astype(HALF)
        slope = gate + (acted - acted * gate) * (2 * root + (6 * root * 0.044715) * square)
        slope_ref[:, cols] = slope.astype(HALF)


def raise_rest(middle, table, weight, acted, slope, after=()):
    rows, width = middle.shape
    wide = weight.shape[-1] // 2

    def kernel(middle_ref, vec_ref, w_ref, acted_in, slope_in, acted_ref, slope_ref):
        row = lambda r: vec_ref[r : r + 1, :]
        gelu_blocks((2, 3), middle_ref, w_ref, row, acted_ref, slope_ref, width, wide)

    ins = [middle, table, weight, acted, slope]
    outs = [held(acted.shape), held(slope.shape)]
    return call(
        kernel,
        (1,),
        whole_specs(ins[:3]) + [pl.BlockSpec(memory_space=pltpu.VMEM)] * 2,
        [pl.BlockSpec(memory_space=pltpu.VMEM)] * 2,
        outs,
        after=after,
        aliases={3: 0, 4: 1},
        cost=0.23125, vmem=10,
    )(*near(*ins))


def lower(place, lens, acted, slope, normed, cotangent, table, group, dims, away, after=()):
    rows, width, seqs = dims
    span = rows // seqs
    n = len(group.arrays)
    tall = 4 * width

    def kernel(place_ref, lens_ref, away_ref, acted_ref, slope_ref, normed_ref, cot_ref, vec_ref, *refs):
        ins = refs[:n]
        act_ref, back_ref, down_ref, up_ref, sums_ref, sent_ref, w_ref, sem = refs[n:]
        sums_ref[...] = jnp.zeros_like(sums_ref)
        group.load(ins, place_ref, w_ref, sem)
        row = lambda r: vec_ref[r : r + 1, :]

        def count(r, value):
            sums_ref[r : r + 1, :] += jnp.sum(value, 0, keepdims=True)

        back_ref[...] = dot(acted_ref[...], columns_of(w_ref, 0, width)) + row(BIAS_DOWN)
        places = lax.broadcasted_iota(jnp.int32, (span, 1), 0)
        for s in range(seqs):
            at = slice(s * span, (s + 1) * span)
            valid = jnp.where(places < lens_ref[s], 1.0, 0.0)
            middle = normed_ref[at, :] * row(GAIN_MID) + row(SHIFT_MID)
            last, inverse = norm_parts(middle + back_ref[at, :])
            act_ref[at, :] = ((last * row(GAIN_LAST) + row(SHIFT_LAST)) * valid).astype(HALF)
            grad = cot_ref[at, :].astype(WIDE) * valid
            count(GAIN_LAST, grad * last)
            count(SHIFT_LAST, grad)
            back = norm_back(grad * row(GAIN_LAST), last, inverse)
            back_ref[at, :] = back
            down = back.astype(HALF)
            down_ref[at, :] = down
            count(BIAS_DOWN, down.astype(WIDE))
        wide = width // 2
        half = down_ref[:, pl.ds(pl.multiple_of(away_ref[0] * wide, 128), wide)]
        for k in range(4):
            cols = slice(k * width, (k + 1) * width)
            sent_ref[cols, :] = dot(acted_ref[:, cols], half, (0, 0)).astype(HALF)
        weight = columns_of(w_ref, 0, width)
        for k in range(4):
            cols = slice(k * width, (k + 1) * width)
            grad = dot(down_ref[...], weight[cols, :], (1, 1))
            up = (grad * slope_ref[:, cols].astype(WIDE)).astype(HALF)
            up_ref[:, cols] = up
            count(BIAS_UP + k, up.astype(WIDE))

    outs = [
        shape((rows, width)),
        held((rows, width), WIDE),
        held((rows, width)),
        held((rows, tall)),
        held((TALL, width), WIDE),
        shape((tall, width // 2)),
    ]
    return call(
        kernel,
        (1,),
        [SCALARS] * 3 + whole_specs([acted, slope, normed, cotangent, table]) + [ANYWHERE] * n,
        whole_specs(outs),
        outs,
        [pltpu.VMEM(group.dims, HALF), pltpu.SemaphoreType.DMA],
        after=after,
        cost=17.7, vmem=18,
    )(place, lens, away, *near(acted, slope, normed), cotangent, *near(table), *far(*group.arrays))


def back_middle(up_grad, back, normed, inverse, table, sums, weight, dims, after=()):
    rows, width = dims
    up = 2 * width
    wide = up + width // 2
    span = 128

    def kernel(up_ref, back_ref, normed_ref, inverse_ref, vec_ref, before_ref, w_ref, first_ref, branch_ref, sums_ref):
        sums_ref[...] = before_ref[...]
        first_ref[...] = dot(up_ref[:, :up], columns_of(w_ref, 0, up), (1, 1))
        first_ref[...] += dot(up_ref[:, up:], columns_of(w_ref, wide, wide + up), (1, 1))
        gain = vec_ref[GAIN_MID : GAIN_MID + 1, :]
        for s in range(rows // span):
            at = slice(s * span, (s + 1) * span)
            grad = back_ref[at, :] + first_ref[at, :]
            normed = normed_ref[at, :]
            sums_ref[GAIN_MID : GAIN_MID + 1, :] += jnp.sum(grad * normed, 0, keepdims=True)
            sums_ref[SHIFT_MID : SHIFT_MID + 1, :] += jnp.sum(grad, 0, keepdims=True)
            first = norm_back(grad * gain, normed, inverse_ref[at, :1])
            first_ref[at, :] = first
            branch = first.astype(HALF)
            branch_ref[at, :] = branch
            sums_ref[BIAS_OUT : BIAS_OUT + 1, :] += jnp.sum(branch.astype(WIDE), 0, keepdims=True)

    outs = [held((rows, width), WIDE), held((rows, width)), held((TALL, width), WIDE)]
    ins = [up_grad, back, normed, inverse, table, sums, weight]
    return call(
        kernel,
        (1,),
        whole_specs(ins),
        whole_specs(outs),
        outs,
        after=after,
        cost=5.1, vmem=8,
    )(*near(*ins))


def back_attend(lens, branch, qkv, stats, sums, weight, dims, low_seq, high_seq, earlier=None, after=()):
    rows, width, seqs = dims
    span = rows // seqs
    pairs = width // 128
    scale = (width // HEADS) ** (-0.5)
    count = high_seq - low_seq
    top = low_seq * span if earlier is not None else 0
    size = (top + count * span, 3 * width)

    def kernel(lens_ref, branch_ref, qkv_ref, stats_ref, before_ref, w_ref, *refs):
        out_ref, sums_ref, mix_ref = refs[-3:]
        sums_ref[...] = before_ref[...]
        if top:
            out_ref[:top, :] = refs[0][...]
        mix_ref[...] = dot(branch_ref[low_seq * span : high_seq * span, :], w_ref[...], (1, 1)).astype(HALF)
        lane = lax.broadcasted_iota(jnp.int32, (span, 128), 1)
        low = lane < 64

        @pl.loop(0, count)
        def _(s):
            here = pl.ds(pl.multiple_of(s * span, span), span)
            at = pl.ds(pl.multiple_of((s + low_seq) * span, span), span)
            there = pl.ds(pl.multiple_of(s * span + top, span), span)
            keep = lane < lens_ref[s + low_seq]
            for p in range(pairs):
                cols = lambda m: slice(m * width + p * 128, m * width + (p + 1) * 128)
                query, grad = qkv_ref[at, cols(0)], mix_ref[here, cols(0)]
                keys = pair_split(qkv_ref[at, cols(1)], low)
                values = pair_split(qkv_ref[at, cols(2)], low)
                scores = dot(query, keys, (1, 1))
                grad_probs = dot(grad, values, (1, 1))
                probs, dscores = [], []
                for h in range(2):
                    half = slice(h * span, (h + 1) * span)
                    lse = stats_ref[at, 2 * p + h : 2 * p + h + 1]
                    prob = jnp.exp(jnp.where(keep, scores[:, half], -1e30) - lse)
                    product = prob * grad_probs[:, half]
                    delta = jnp.sum(product, -1, keepdims=True)
                    probs.append(prob.astype(HALF))
                    dscores.append((product - prob * delta).astype(HALF))
                probs = jnp.concatenate(probs, axis=1)
                dscores = jnp.concatenate(dscores, axis=1)
                dvalues = dot(probs, grad, (0, 0))
                dkeys = dot(dscores, query, (0, 0))
                dquery = (dot(dscores, keys).astype(HALF).astype(WIDE) * scale).astype(HALF)
                out_ref[there, cols(0)] = dquery
                sums_ref[BIAS_Q : BIAS_Q + 1, cols(0)] += jnp.sum(dquery.astype(WIDE), 0, keepdims=True)
                dkeys = jnp.where(low, dkeys[:span], dkeys[span:]).astype(HALF)
                out_ref[there, cols(1)] = dkeys
                dvalues = jnp.where(low, dvalues[:span], dvalues[span:]).astype(HALF)
                out_ref[there, cols(2)] = dvalues
                sums_ref[BIAS_V : BIAS_V + 1, cols(0)] += jnp.sum(dvalues.astype(WIDE), 0, keepdims=True)

    ins = [branch, qkv, stats, sums, weight] + ([earlier] if top else [])
    outs = [held(size), held((TALL, width), WIDE)]
    return call(
        kernel,
        (1,),
        [SCALARS] + whole_specs(ins),
        whole_specs(outs),
        outs,
        [pltpu.VMEM((count * span, width), HALF)],
        after=after,
        cost=7.5, vmem=6,
    )(lens, *near(*ins))


def back_start(bounds, place, dproj, first, feats, sums, weight, dims, shards, after=()):
    rows, width, seqs = dims
    span = rows // seqs
    half = 3 * width // 2
    wide = half + TFREQ

    def kernel(bounds_ref, place_ref, dproj_ref, first_ref, feats_ref, sums_ref, w_ref, hidden_ref, *refs):
        acc_ref, temb_ref = refs[-2:]
        more_ref = refs[0]
        acc_ref[...] = dot(dproj_ref[:, :half], columns_of(w_ref, 0, half), (1, 1))
        acc_ref[...] += dot(dproj_ref[:, half:], columns_of(w_ref, wide, wide + half), (1, 1))
        temb_ref[...] = jnp.zeros_like(temb_ref)
        places = lax.broadcasted_iota(jnp.int32, (span, 1), 0)
        for s in range(seqs):
            at = slice(s * span, (s + 1) * span)
            grad = acc_ref[at, :] + first_ref[at, :]
            hidden_ref[at, :] = grad.astype(HALF)
            target = jnp.where(places >= bounds_ref[s], 1.0, 0.0)
            temb_ref[s : s + 1, :] = jnp.sum(grad * target, 0, keepdims=True)
        grad = lax.dot_general(
            temb_ref[...],
            feats_ref[...].astype(WIDE),
            (((0,), (0,)), ((), ())),
            precision=lax.Precision.HIGHEST,
            preferred_element_type=WIDE,
        )
        if not shards:
            more_ref[...] = grad
            return
        grad = grad.astype(HALF)
        pieces = pieces_of(sums_ref[...].astype(HALF), width, shards).reshape(shards, TALL, TFREQ)
        rest = jnp.zeros((shards, width // shards - TALL, TFREQ), HALF)
        pieces = jnp.concatenate([pieces, rest], axis=1).reshape(width, TFREQ)
        first_half = place_ref[3] == 0
        more_ref[...] = jnp.where(first_half, grad, pieces)
        refs[1][...] = jnp.where(first_half, pieces, grad)

    outs = [shape((rows, width))]
    outs += [held((width, TFREQ)), shape((width, TFREQ))] if shards else [shape((width, TFREQ), WIDE)]
    ins = [dproj, first, feats, sums, weight]
    return call(
        kernel,
        (1,),
        [SCALARS, SCALARS] + whole_specs(ins),
        whole_specs(outs),
        outs,
        [pltpu.VMEM((rows, width), WIDE), pltpu.VMEM(feats.shape[:1] + (width,), WIDE)],
        after=after,
        token=True,
        cost=5.7, vmem=8,
    )(bounds, place, *near(dproj, first), feats, *near(sums, weight))


def half_of(ref, half):
    wide = ref.shape[1] // 2
    return ref[:, pl.ds(pl.multiple_of(half * wide, 128), wide)]


def outer(half, pairs, extras=None, after=()):
    columns = [r.shape[1] // 2 for _, r in pairs]
    tall = pairs[0][0].shape[1]
    wide_all = sum(columns) + (TFREQ if extras is not None else 0)

    def kernel(half_ref, *refs):
        out_ref, low = refs[-1], 0
        for n, wide in enumerate(columns):
            right = half_of(refs[2 * n + 1], half_ref[0])
            out_ref[:, low : low + wide] = dot(refs[2 * n][...], right, (0, 0)).astype(HALF)
            low += wide
        if extras is not None:
            out_ref[:, low:] = refs[-2][...]

    ins = sum([[l, r] for l, r in pairs], [])
    rest = [extras] if extras is not None else []
    return call(
        kernel,
        (1,),
        whole_specs(ins + rest),
        fixed((tall, wide_all)),
        shape((tall, wide_all)),
        prefetch=(half,),
        after=after,
        cost=2.8, vmem=8,
    )(*near(*ins), *rest)


def keep_outer(half, spot, pairs, arrived, zs, extras=None, after=()):
    columns = [r.shape[1] // 2 for _, r in pairs]
    tall = pairs[0][0].shape[1]
    wide = sum(columns) + (TFREQ if extras is not None else 0)
    each = tall // (zs * XS * 2)
    low_zs = zs // 2
    count = len(pairs)

    def kernel(half_ref, spot_ref, *refs):
        ins, refs = refs[: 2 * count], refs[2 * count :]
        arrived_ref, refs = refs[0], refs[1:]
        if extras is not None:
            more_ref, refs = refs[0], refs[1:]
        outs, value_ref, sems = refs[:5], refs[5], refs[6]
        x0, y0 = spot_ref[1], spot_ref[2]

        def put(value, low, high):
            value_ref[..., low:high] = value.astype(HALF).reshape(zs, XS, 2, each, high - low)

        low = 0
        for n, high in enumerate(columns):
            high += low
            right = half_of(ins[2 * n + 1], half_ref[0])
            put(dot(ins[2 * n][...], right, (0, 0)) + arrived_ref[:, low:high].astype(WIDE), low, high)
            low = high
        if extras is not None:
            put(more_ref[...].astype(WIDE) + arrived_ref[:, low:].astype(WIDE), low, low + TFREQ)
        own, by_x, by_y, x_later, y_later = outs
        rest = zs - low_zs
        lows, highs = pl.ds(0, low_zs), pl.ds(low_zs, rest)
        x1, y1 = 1 - x0, 1 - y0
        moves = [
            ((pl.ds(0, zs), x0, y0), own),
            ((lows, x1, y1), by_x.at[pl.ds(0, low_zs)]),
            ((lows, x1, y0), by_x.at[pl.ds(low_zs, low_zs)]),
            ((highs, x1, y1), by_y.at[pl.ds(0, rest)]),
            ((highs, x0, y1), by_y.at[pl.ds(rest, rest)]),
            ((highs, x1, y0), x_later),
            ((lows, x0, y1), y_later),
        ]
        load([pltpu.make_async_copy(value_ref.at[cut], o, sems.at[n]) for n, (cut, o) in enumerate(moves)])

    ins = sum([[l, r] for l, r in pairs], [])
    rest = [arrived] + ([extras] if extras is not None else [])
    sizes = [(k, each, wide) for k in (zs, 2 * low_zs, 2 * (zs - low_zs), zs - low_zs, low_zs)]
    return call(
        kernel,
        (1,),
        whole_specs(ins + rest),
        [ANYWHERE] * len(sizes),
        [shape(s) for s in sizes],
        [pltpu.VMEM((zs, XS, 2, each, wide), HALF), pltpu.SemaphoreType.DMA((7,))],
        prefetch=(half, spot),
        after=after,
        token=True,
        cost=4.3, vmem=14,
    )(*near(*ins), *rest)


def plain_outer(left, right):
    return dot(left, right, (0, 0)).astype(HALF)


class Routes:
    def __init__(self, shards, reps):
        self.shards, self.reps, self.zs = shards, reps, shards // XS

    def core(self, value):
        return lax.ppermute(value, "rep", [(r, r ^ 1) for r in range(self.reps)])

    def y(self, value):
        return lax.ppermute(value, "rep", [(r, r ^ 2) for r in range(self.reps)])

    def x(self, value):
        return lax.ppermute(value, "fsdp", [(f, f ^ 1) for f in range(self.shards)])

    def shift(self, value, step):
        return lax.ppermute(value, "fsdp", [(f, (f + step * XS) % self.shards) for f in range(self.shards)])

    def z(self, value):
        lines = [[z * XS + x for z in range(self.zs)] for x in range(XS)]
        return lax.all_to_all(value, "fsdp", 0, 0, axis_index_groups=lines, tiled=True)


def z(self, value, step):
        return lax.ppermute(
            value, "fsdp", [(f, (f + step * XS) % self.shards) for f in range(self.shards)]
        )


def prepare(spot, qkv, time, small, up, out, down, zs):
    cut, part = qkv.shape[0] // 2, qkv.shape[0]
    tall = down.shape[0] // 2
    third = down.shape[1] // 2
    halves = [v.shape[1] // 2 for v in (qkv, up, out)]
    widths = [halves[0] + TFREQ, halves[1] + halves[2], tall // cut * third]
    n = len(small)

    def kernel(spot_ref, qkv_ref, time_ref, up_ref, out_ref, down_ref, *refs):
        vecs, outs, table_ref, kept, sem = refs[:n], refs[n : n + 3], refs[n + 3], refs[n + 4 : -1], refs[-1]
        load([pltpu.make_async_copy(v, h, sem.at[i]) for i, (v, h) in enumerate(zip(vecs, kept))])
        table_ref[...] = jnp.zeros_like(table_ref)
        top = 0
        for ref in kept:
            value = ref[...].astype(WIDE).reshape(1, ref.shape[0])
            for m in range(ref.shape[0] // part):
                table_ref[top : top + 1, :part] = value[:, m * part : (m + 1) * part]
                top += 1
        table = jnp.where(spot_ref[2] == 0, table_ref[...], 0.0).astype(HALF)
        first = [qkv_ref[...], jnp.where(spot_ref[3] == 0, time_ref[...], table)]
        third_parts = [down_ref[i * cut : (i + 1) * cut, :] for i in range(tall // cut)]
        for ref, parts in zip(outs, (first, [up_ref[...], out_ref[...]], third_parts)):
            here = 0
            for value in parts:
                there = slice(here, here + value.shape[1])
                if len(ref.shape) == 2:
                    ref[:, there] = value
                else:
                    for k in range(zs):
                        ref[k, :, there] = value
                here += value.shape[1]

    quarter = lambda rows, columns: pl.BlockSpec((rows, columns), lambda i, spot: (spot[2], spot[3]))
    sizes = [(zs, cut, w) if at_once else (cut, w) for w, at_once in zip(widths, (False, False, False))]
    return call(
        kernel,
        (1,),
        [
            quarter(cut, halves[0]),
            pl.BlockSpec((cut, TFREQ), lambda i, spot: (spot[2], 0)),
            quarter(cut, halves[1]),
            quarter(cut, halves[2]),
            quarter(tall, third),
        ]
        + [ANYWHERE] * n,
        [fixed(s) for s in sizes],
        [shape(s) for s in sizes],
        [pltpu.VMEM((cut, TFREQ), WIDE)]
        + [pltpu.VMEM(v.shape, HALF) for v in small]
        + [pltpu.SemaphoreType.DMA((n,))],
        prefetch=(spot,),
        cost=0.1875, vmem=6,
    )(*far(qkv, time, up, out, down, *small))


def weave(spot, zs, arrays, outs, after=()):
    arrays = list(arrays)

    def kernel(spot_ref, *refs):
        for ref, (copies, parts) in zip(refs[len(arrays) :], outs):
            here = 0
            for n, low, count, step in parts:
                cols = slice(low, low + count)
                value = refs[n][:, cols] if step is None else refs[n][lax.rem(spot_ref[0] + (zs - step), zs), :, cols]
                there = slice(here, here + count)
                if copies is None:
                    ref[:, there] = value
                else:
                    for k in range(copies):
                        ref[k, :, there] = value
                here += count

    rows = arrays[0].shape[-2]
    sizes = [(() if c is None else (c,)) + (rows, sum(p[2] for p in parts)) for c, parts in outs]
    return call(
        kernel,
        (1,),
        [SCALARS] + whole_specs(arrays),
        [fixed(s) for s in sizes],
        [shape(s) for s in sizes],
        after=after,
        cost=0.05, vmem=8,
    )(spot, *arrays)


def cut_of(layout, low, high, dx, dy):
    out, left = [], 0
    for g, dz, count in layout:
        first, last = max(low, left), min(high, left + count)
        if first < last:
            out.append((g, dz, dx, dy, first - left, last - first))
        left += count
    return out


def middle_of(count):
    return count // 2 // 128 * 128


class Gather:
    def __init__(self, spot, owns, routes):
        self.spot, self.routes = spot, routes
        self.widths = [o.shape[-1] for o in owns]
        self.arrays, self.segments = [], [[] for _ in self.widths]
        shifts = lambda o: [o] + [routes.shift(o, step) for step in range(1, routes.zs)]
        self.by_z = [shifts(o) if o.ndim == 2 else [routes.z(o)] for o in owns]
        self.line = [None] * len(owns)

    def weave(self, arrays, outs, after=()):
        return weave(self.spot, self.routes.zs, arrays, outs, after)

    def add(self, array, parts, dc=0):
        low = 0
        for g, dz, dx, dy, column, count in parts:
            self.segments[g].append((len(self.arrays), low, count, dz, dx, dy, dc, column))
            low += count
        self.arrays.append(array)

    def both(self, array, parts):
        core = self.routes.core(array)
        self.add(array, parts)
        self.add(core, parts, 1)
        return core

    def group(self, g, dims):
        used = sorted({s[0] for s in self.segments[g]})
        segments = [(used.index(s[0]),) + s[1:] for s in self.segments[g]]
        return Gathered([self.arrays[n] for n in used], segments, dims)

    def follow(self, g, after=()):
        come, width = self.by_z[g], self.widths[g]
        if len(come) > 1:
            lines = [(step, 0, width, None) for step in range(self.routes.zs)]
        else:
            lines = [(0, 0, width, step) for step in range(self.routes.zs)]
        (line,) = self.weave(come, [(None, lines)], after)
        self.line[g] = [line, self.routes.x(line), self.routes.y(line)]
        return line

    def onward(self, g, after=()):
        whole = [(g, step, self.widths[g]) for step in range(self.routes.zs)]
        count = self.routes.zs * self.widths[g]
        cut = middle_of(count)
        x2, y2, known = self.weave(
            self.line[g],
            [
                (None, [(2, 0, cut, None)]),
                (None, [(1, cut, count - cut, None)]),
                (None, [(k, 0, count, None) for k in range(3)]),
            ],
            after,
        )
        sent = x2
        x2, y2 = self.routes.x(x2), self.routes.y(y2)
        self.both(known, sum([cut_of(whole, 0, count, dx, dy) for dx, dy in ((0, 0), (1, 0), (0, 1))], []))
        self.both(x2, cut_of(whole, 0, cut, 1, 1))
        self.both(y2, cut_of(whole, cut, count, 1, 1))
        self.passed = [x2, y2]
        return sent


def total(*terms):
    return functools.reduce(lambda a, b: a + b, [t.astype(WIDE) for t in terms]).astype(HALF)


def first_hop(kept, routes):
    own, by_x, by_y, x_later, y_later = kept[:5]
    return own, routes.x(by_x), routes.y(by_y), x_later, y_later


def second_hop(state, routes, after=()):
    own, from_x, from_y, x_later, y_later = state
    rest, low = x_later.shape[0], y_later.shape[0]

    def kernel(from_x_ref, from_y_ref, x_ref, y_ref, x_out, y_out):
        x_out[...] = total(x_ref[...], from_y_ref[:rest])
        y_out[...] = total(y_ref[...], from_x_ref[:low])

    ins = (from_x, from_y, x_later, y_later)
    outs = [shape(x_later.shape), shape(y_later.shape)]
    x_later, y_later, token = call(kernel, (1,), whole_specs(ins), whole_specs(outs), outs, after=after, cost=0.5, vmem=6, token=True)(*ins)
    return own, from_x, from_y, routes.x(x_later), routes.y(y_later), token


def line_sum(spot, state, after=()):
    state = state[:5]
    own, _, _, x_late, y_late = state
    zs, rows, columns = own.shape
    low, rest = y_late.shape[0], x_late.shape[0]

    def kernel(spot_ref, own_ref, from_x, from_y, x_late, y_late, *refs):
        outs, line_ref = refs[:-1], refs[-1]
        line_ref[:low] = total(own_ref[:low], from_x[low:], y_late[...])
        line_ref[low:] = total(own_ref[low:], x_late[...], from_y[rest:])
        for step in range(zs):
            outs[step][...] = line_ref[lax.rem(spot_ref[0] + step, zs)]

    return call(
        kernel,
        (1,),
        [SCALARS] + whole_specs(state),
        [fixed((rows, columns))] * zs,
        [shape((rows, columns))] * zs,
        [pltpu.VMEM(own.shape, HALF)],
        after=after,
        cost=0.5,
        vmem=8,
        token=True,
    )(spot, *state)


def last_hops(terms, routes, after=()):
    ins = [terms[0]] + [routes.shift(v, step) for step, v in enumerate(terms[:-1]) if step]

    def kernel(*refs):
        refs[-1][...] = total(*[r[...] for r in refs[:-1]])

    size = ins[0].shape
    mine, token = call(
        kernel, (1,), whole_specs(ins), [fixed(size)], [shape(size)], after=after, cost=0.5, vmem=4, token=True
    )(*ins)
    other = routes.y(mine)
    return [mine, routes.core(mine), other, routes.core(other)], token


def in_order(pieces, y0, c0):
    rows = [
        [jnp.where(c0 == 0, a, b), jnp.where(c0 == 0, b, a)] for a, b in (pieces[0:2], pieces[2:4])
    ]
    return [
        [jnp.where(y0 == 0, rows[y][c], rows[1 - y][c]) for c in range(2)] for y in range(2)
    ]


def finish(spot, pieces, cuts, outs, vectors=(), after=()):
    rows = pieces[0].shape[0]
    count = len(outs)

    def kernel(spot_ref, *refs):
        ins, dests, small = refs[:4], refs[4 : 4 + count], refs[4 + count :]
        grid = in_order([r[...] for r in ins], spot_ref[2], spot_ref[3])
        for y in range(2):
            for c, low, wide, out, column in cuts:
                dests[out][y * rows : (y + 1) * rows, column : column + wide] = grid[y][c][
                    :, low : low + wide
                ].astype(WIDE)
        top = 0
        if small:
            table = grid[0][1][:TALL, -TFREQ:].astype(WIDE)
        for ref in small:
            each = vectors[0]
            n = ref.shape[0] // each
            parts = [table[r : r + 1, :each] for r in range(top, top + n)]
            ref[...] = jnp.concatenate(parts, axis=1).reshape(n * each)
            top += n

    lengths = list(vectors[1]) if vectors else []
    return call(
        kernel,
        (1,),
        [SCALARS] + [fixed(v.shape) for v in pieces],
        [fixed(o) for o in outs] + [fixed((n,)) for n in lengths],
        [shape(o, WIDE) for o in outs] + [shape((n,), WIDE) for n in lengths],
        after=after,
        token=True,
        cost=1.7, vmem=12,
    )(spot, *pieces)


def pair_split(value, low):
    zero = jnp.zeros_like(value)
    return jnp.concatenate([jnp.where(low, value, zero), jnp.where(low, zero, value)], axis=0)


def time_features(timesteps):
    half = TFREQ // 2
    freqs = jnp.exp(-math.log(10000.0) * jnp.arange(half).astype(WIDE) / half)
    angles = timesteps.astype(WIDE)[:, None] * freqs[None, :]
    return jnp.concatenate([jnp.cos(angles), jnp.sin(angles)], axis=1)


def layer(
    hidden,
    cotangent,
    lengths,
    bounds,
    timesteps,
    weight_qkv,
    bias_qv,
    weight_out,
    bias_out,
    gain_mid,
    shift_mid,
    weight_up,
    bias_up,
    weight_down,
    bias_down,
    gain_last,
    shift_last,
    weight_time,
):
    shards, reps = lax.axis_size("fsdp"), lax.axis_size("rep")
    rows, width = hidden.shape
    seqs = lengths.shape[0]
    part = weight_out.shape[0]
    by_hand = reps == 4 and shards == 8 and part == 96
    rep, shard = lax.axis_index("rep"), lax.axis_index("fsdp")
    spot = jnp.stack([shard // XS, shard % XS, rep // 2, rep % 2]).astype(jnp.int32)
    small = [bias_qv, bias_out, gain_mid, shift_mid, bias_up, bias_down, gain_last, shift_last]
    feats = jnp.pad(time_features(timesteps).astype(HALF), ((0, -seqs % 8), (0, 0)))
    half, out = 3 * width // 2, width // 2
    known = None
    if by_hand:
        routes = Routes(shards, reps)
        zs = routes.zs
        owns = prepare(spot, weight_qkv, weight_time, small, weight_up, weight_out, weight_down, zs)
        gather = Gather(spot, owns, routes)
        places, cut = (zs, XS, 2), part // 2
        gather.follow(0)
        gather.onward(0, gather.by_z[1])
        sent = gather.follow(1, gather.passed)
        group1 = gather.group(0, places + (cut, 2 * gather.widths[0]))
    else:
        whole = lambda v: lax.all_gather(v, "fsdp", axis=0, tiled=True)
        qkv, up, output = whole(weight_qkv), whole(weight_up), whole(weight_out)
        blank = jnp.zeros((width, TFREQ), HALF)
        group1 = Whole(jnp.concatenate([qkv[:, :half], blank, qkv[:, half:], blank], axis=1))
        group2 = Whole(
            jnp.concatenate([up[:, : 2 * width], output[:, :out], up[:, 2 * width :], output[:, out:]], axis=1)
        )
        group3 = Whole(whole(weight_down))
        table = jnp.concatenate([whole(v).reshape(-1, width) for v in small]).astype(WIDE)
        known = (whole(weight_time), jnp.pad(table, ((0, TALL - table.shape[0]), (0, 0))))

    per_seq, flat = (rows, width, seqs), (rows, width)
    start_b, qkv, table, time, whole1 = project(
        spot, bounds, hidden, feats, group1, known, per_seq, after=[sent] if by_hand else ()
    )
    mixed, stats = attend(lengths, qkv, per_seq)
    if by_hand:
        sent = gather.follow(2, [gather.onward(1, [mixed] + gather.by_z[2])])
        group2 = gather.group(1, places + (cut, 2 * gather.widths[1]))
    normed, middle, inverse, acted, slope, whole_out, whole2 = raise_up(
        spot, bounds, hidden, feats, time, mixed, table, group2, per_seq, after=[sent] if by_hand else ()
    )
    if by_hand:
        sent = gather.onward(2, [middle])
        group3 = gather.group(2, places + (weight_down.shape[0] // 2, width))
    acted, slope = raise_rest(middle, table, whole2, acted, slope, after=[sent] if by_hand else ())
    mine, away = spot[3:], 1 - spot[3:]
    activations, back, down, up_grad, sums, sent = lower(
        spot, lengths, acted, slope, normed, cotangent, table, group3, per_seq, away
    )
    first, branch, sums = back_middle(up_grad, back, normed, inverse, table, sums, whole2, flat)
    if by_hand:
        kept3 = keep_outer(mine, spot, [(acted, down)], routes.core(sent), zs, after=[branch])
        pairs2 = [(middle, up_grad), (mixed, branch)]
        sent = outer(away, pairs2, after=[kept3[-1]])
        early, sums = back_attend(
            lengths, branch, qkv, stats, sums, whole_out, per_seq, 0, seqs // 2, after=[sent]
        )
        kept2 = keep_outer(mine, spot, pairs2, routes.core(sent), zs, after=[early])
        dproj, sums = back_attend(
            lengths, branch, qkv, stats, sums, whole_out, per_seq, seqs // 2, seqs, early, after=[kept2[-1]]
        )
        state3 = second_hop(first_hop(kept3, routes), routes, after=[dproj])
    else:
        dproj, sums = back_attend(lengths, branch, qkv, stats, sums, whole_out, per_seq, 0, seqs)
    grad_hidden, extras, *more, done = back_start(
        bounds, spot, dproj, first, feats, sums, whole1, per_seq, shards if by_hand else 0, after=[state3[-1]] if by_hand else ()
    )
    if by_hand:
        state2 = second_hop(first_hop(kept2, routes), routes, after=[done])
        sent = outer(away, [(start_b, dproj)], more[0], after=[state2[-1]])
        terms3 = line_sum(spot, state3, after=[sent])
        kept1 = keep_outer(
            mine, spot, [(start_b, dproj)], routes.core(sent), zs, extras, after=[terms3[-1]]
        )
        terms2 = line_sum(spot, state2, after=[kept1[-1]])
        sums3, token = last_hops(terms3, routes, after=[terms2[-1]])
        state1 = second_hop(first_hop(kept1, routes), routes, after=[token])
        out_down, token = finish(
            spot, sums3, [(c, 0, out, 0, c * out) for c in range(2)], [weight_down.shape], after=[state1[-1]]
        )
        terms1 = line_sum(spot, state1, after=[token])
        sums2, token = last_hops(terms2, routes, after=[terms1[-1]])
        out_up, out_out, token = finish(
            spot,
            sums2,
            [(c, 0, 2 * width, 0, c * 2 * width) for c in range(2)]
            + [(c, 2 * width, out, 1, c * out) for c in range(2)],
            [weight_up.shape, weight_out.shape],
            after=[token],
        )
        sums1, _ = last_hops(terms1, routes, after=[])
        out_qkv, out_time, *out_small, _ = finish(
            spot,
            sums1,
            [(c, 0, half, 0, c * half) for c in range(2)] + [(0, half, TFREQ, 1, 0)],
            [weight_qkv.shape, weight_time.shape],
            (part, [v.shape[0] for v in small]),
        )
    else:

        def summed(v):
            v = lax.psum_scatter(v.astype(HALF), "fsdp", scatter_dimension=0, tiled=True)
            return lax.psum(v, "rep").astype(WIDE)

        out_qkv, out_out = summed(plain_outer(start_b, dproj)), summed(plain_outer(mixed, branch))
        out_up, out_down = summed(plain_outer(middle, up_grad)), summed(plain_outer(acted, down))
        out_time = summed(extras)
        counts = [v.shape[0] * shards // width for v in small]
        tops = [sum(counts[:i]) for i in range(len(counts))]
        out_small = [summed(sums[t : t + n].reshape(-1)) for t, n in zip(tops, counts)]
    return (
        activations,
        grad_hidden,
        out_qkv,
        out_small[0],
        out_out,
        out_small[1],
        out_small[2],
        out_small[3],
        out_up,
        out_small[4],
        out_down,
        out_small[5],
        out_small[6],
        out_small[7],
        out_time,
    )


def solution(mesh):
    tokens, table, vector = P(("rep", "fsdp"), None), P("fsdp", None), P("fsdp")
    per_sequence = P(("rep", "fsdp"))
    weights = (table, vector, table, vector, vector, vector, table, vector, table, vector, vector, vector, table)
    return jax.shard_map(
        layer,
        mesh=mesh,
        in_specs=(tokens, tokens, per_sequence, per_sequence, per_sequence) + weights,
        out_specs=(tokens, tokens) + weights,
        check_vma=False,
    )
```

profile of v0, /device:TPU:1, one launch (start us, length us, event | category | flops | bytes accessed | tf_op | source)
XLA Modules:
  0.0 248.8 jit_solution(6538774389669483976)
XLA Ops:
  0.8 2.6 %shard_map.289 = (bf16[48,1280]{1,0:T(8,128)(2,1)S(1)}, bf16[48,1920]{1,0:T(8,128)(2,1)S(1)}, bf16[48,1536]{1,0:T(8,128)(2,1)S(1)}) custom-call(s32[4]{0:T(128)S(1)} %pad_add_fusion.refs_0_.refs_1_, bf16[96,2304]{1,0:T(8,128)(2,1)} %refs_1_.4, bf16[96,128]{1,0:T(8,128)(2,1)} %refs_2_.3, bf16[96,3072]{1,0:T(8,128)(2,1)} %refs_3_.1, bf16[96,768]{1,0:T(8,128)(2,1)} %refs_4_.1, ...), custom_call_target="tpu_custom_call" | custom-call | flops 750000000 | bytes 750000 | tf_op jit(solution)/shard_map/pallas_call | solution.py:69
  3.3 4.2 %collective-permute-start.2 = (bf16[48,1280]{1,0:T(8,128)(2,1)S(1)}, bf16[48,1280]{1,0:T(8,128)(2,1)S(1)}, u32[]{:S(2)}, u32[]{:S(2)}) collective-permute-start(bf16[48,1280]{1,0:T(8,128)(2,1)S(1)} %get-tuple-element.121.refs_1_), channel_id=1, source_target_pairs={{0,6},{1,7},{2,0},{3,1},{4,2},{5,3},{6,4},{7,5},{8,14},{9,15},{10,... | collective-permute-start | bytes 368648 | tf_op jit(solution)/shard_map/ppermute | solution.py:710
  9.4 8.5 %collective-permute-done.1.refs_3_ = bf16[48,1280]{1,0:T(8,128)(2,1)S(1)} collective-permute-done((bf16[48,1280]{1,0:T(8,128)(2,1)S(1)}, bf16[48,1280]{1,0:T(8,128)(2,1)S(1)}, u32[]{:S(2)}, u32[]{:S(2)}) %collective-permute-start.1) | collective-permute-done | bytes 122912 | tf_op jit(solution)/shard_map/ppermute | solution.py:710
  25.7 12.1 %collective-permute-done.6.refs_6_.refs_3_ = bf16[48,1920]{1,0:T(8,128)(2,1)S(1)} collective-permute-done((bf16[48,1920]{1,0:T(8,128)(2,1)S(1)}, bf16[48,1920]{1,0:T(8,128)(2,1)S(1)}, u32[]{:S(2)}, u32[]{:S(2)}) %collective-permute-start.6) | collective-permute-done | bytes 184352 | tf_op jit(solution)/shard_map/ppermute | solution.py:710
  38.5 2.8 %collective-permute-start.8 = (bf16[48,15360]{1,0:T(8,128)(2,1)S(1)}, bf16[48,15360]{1,0:T(8,128)(2,1)S(1)}, u32[]{:S(2)}, u32[]{:S(2)}) collective-permute-start(bf16[48,15360]{1,0:T(8,128)(2,1)S(1)} %get-tuple-element.123.refs_4_), channel_id=1, source_target_pairs={{0,8},{8,0},{16,24},{24,16},{1,9},{9,1},{17,25},{25,17},{2,10},{10... | collective-permute-start | bytes 4423688 | tf_op jit(solution)/shard_map/ppermute | solution.py:701
  41.9 7.0 %collective-permute-done.9.refs_5_.refs_6_ = bf16[48,2560]{1,0:T(8,128)(2,1)S(1)} collective-permute-done((bf16[48,2560]{1,0:T(8,128)(2,1)S(1)}, bf16[48,2560]{1,0:T(8,128)(2,1)S(1)}, u32[]{:S(2)}, u32[]{:S(2)}) %collective-permute-start.9) | collective-permute-done | bytes 245792 | tf_op jit(solution)/shard_map/ppermute | solution.py:707
  55.9 7.0 %shard_map.293 = (bf16[768,768]{1,0:T(8,128)(2,1)S(1)}, bf16[768,2304]{1,0:T(8,128)(2,1)S(1)}, f32[16,768]{1,0:T(8,128)S(1)}, bf16[768,128]{1,0:T(8,128)(2,1)S(1)}, bf16[4,2,2,48,2560]{4,3,2,1,0:T(8,128)(2,1)S(1)}) custom-call(s32[4]{0:T(128)S(1)} %pad_add_fusion.refs_0_.refs_1_, s32[6]{0:T(128)S(1)} %copy-done.6, bf16[768,768]{1,0:T(8,128)(2,1)S(1)} %copy-done.1, ...), custom_call_target="tpu_custom_call" | custom-call | flops 1750000000 | bytes 1750000 | tf_op jit(solution)/shard_map/pallas_call | solution.py:69
  63.0 7.2 %shard_map.294 = (bf16[768,768]{1,0:T(8,128)(2,1)S(1)}, f32[768,128]{1,0:T(8,128)S(1)}) custom-call(s32[6]{0:T(128)S(1)} %copy-done.11, bf16[768,2304]{1,0:T(8,128)(2,1)S(1)} %get-tuple-element.127.refs_1_.refs_2_), custom_call_target="tpu_custom_call" | custom-call | flops 1750000000 | bytes 1750000 | tf_op jit(solution)/shard_map/pallas_call | solution.py:69
  75.8 6.6 %collective-permute-done.21.refs_11_ = bf16[48,3840]{1,0:T(8,128)(2,1)S(1)} collective-permute-done((bf16[48,3840]{1,0:T(8,128)(2,1)S(1)}, bf16[48,3840]{1,0:T(8,128)(2,1)S(1)}, u32[]{:S(2)}, u32[]{:S(2)}) %collective-permute-start.21) | collective-permute-done | bytes 368672 | tf_op jit(solution)/shard_map/ppermute | solution.py:704
  88.1 8.7 %shard_map.297 = (f32[768,768]{1,0:T(8,128)S(1)}, bf16[768,768]{1,0:T(8,128)(2,1)S(1)}, f32[768,128]{1,0:T(8,128)S(1)}, bf16[768,3072]{1,0:T(8,128)(2,1)S(1)}, b...) custom-call(s32[4]{0:T(128)S(1)} %pad_add_fusion.refs_0_.refs_1_, ...), custom_call_target="tpu_custom_call" | custom-call | flops 2175000064 | bytes 2175000 | tf_op jit(solution)/shard_map/pallas_call | solution.py:69
  98.4 8.0 %collective-permute-done.28.refs_12_ = bf16[48,3072]{1,0:T(8,128)(2,1)S(1)} collective-permute-done((bf16[48,3072]{1,0:T(8,128)(2,1)S(1)}, bf16[48,3072]{1,0:T(8,128)(2,1)S(1)}, u32[]{:S(2)}, u32[]{:S(2)}) %collective-permute-start.28) | collective-permute-done | bytes 294944 | tf_op jit(solution)/shard_map/ppermute | solution.py:704
  107.6 3.6 %shard_map.299 = (bf16[768,3072]{1,0:T(8,128)(2,1)S(1)}, bf16[768,3072]{1,0:T(8,128)(2,1)S(1)}) custom-call(bf16[768,768]{1,0:T(8,128)(2,1)S(1)} %get-tuple-element.134.refs_4_.refs_0_.refs_1_.refs_2_, f32[16,768]{1,0:T(8,128)S(1)} %get-tuple-element.129.refs_6_.refs_1_.refs_7_.refs_4_, ...), custom_call_target="tpu_custom_call", output_to_operand_aliasing={{0}: (3, {}), {1}: (4, {})} | custom-call | flops 925000000 | bytes 925000 | tf_op jit(solution)/shard_map/pallas_call | solution.py:69
  112.7 17.9 %shard_map.300 = (bf16[768,768]{1,0:T(8,128)(2,1)}, f32[768,768]{1,0:T(8,128)S(1)}, bf16[768,768]{1,0:T(8,128)(2,1)S(1)}, bf16[768,3072]{1,0:T(8,128)(2,1)S(1)},...) custom-call(s32[4]{0:T(128)S(1)} %pad_add_fusion.refs_0_.refs_1_, s32[6]{0:T(128)S(1)} %copy-done.11, ...), custom_call_target="tpu_custom_call" | custom-call | flops 70799998976 | bytes 70800000 | tf_op jit(solution)/shard_map/pallas_call | solution.py:69
  131.0 5.2 %shard_map.301 = (f32[768,768]{1,0:T(8,128)S(1)}, bf16[768,768]{1,0:T(8,128)(2,1)S(1)}, f32[16,768]{1,0:T(8,128)S(1)}) custom-call(bf16[768,3072]{1,0:T(8,128)(2,1)S(1)} %get-tuple-element.145.refs_0_.refs_2_.refs_3_, f32[768,768]{1,0:T(8,128)S(1)} %get-tuple-element.146.refs_1_, f32[768,768]{1,0:T(8,128)S(1)} %get-tuple-element.141.refs_5_.refs_2_, ...), custom_call_target="tpu_custom_call" | custom-call | flops 20400001024 | bytes 20400000 | tf_op jit(solution)/shard_map/pallas_call | solution.py:69
  136.2 3.6 %shard_map.302 = (bf16[4,192,384]{2,1,0:T(8,128)(2,1)S(1)}, bf16[4,192,384]{2,1,0:T(8,128)(2,1)S(1)}, bf16[4,192,384]{2,1,0:T(8,128)(2,1)S(1)}, bf16[2,192,384]{...) custom-call(s32[1]{0:T(128)} %bitcast.3.refs_0_, s32[4]{0:T(128)S(1)} %pad_add_fusion.refs_0_.refs_1_, ...), custom_call_target="tpu_custom_call" | custom-call | flops 17200001024 | bytes 17200000 | tf_op jit(solution)/shard_map/pallas_call | solution.py:69
  139.8 2.6 %shard_map.303.refs_6_ = bf16[768,1920]{1,0:T(8,128)(2,1)S(1)} custom-call(s32[1]{0:T(128)S(6)} %sub.12.refs_2_.refs_0_, bf16[768,768]{1,0:T(8,128)(2,1)S(1)} %get-tuple-element.134.refs_4_.refs_0_.refs_1_.refs_2_, bf16[768,3072]{1,0:T(8,128)(2,1)S(1)} %get-tuple-element.145.refs_0_.refs_2_.refs_3_, ...), custom_call_target="tpu_custom_call" | custom-call | flops 11200000000 | bytes 11200000 | tf_op jit(solution)/shard_map/pallas_call | solution.py:69
  144.3 7.4 %shard_map.304 = (bf16[384,2304]{1,0:T(8,128)(2,1)S(1)}, f32[16,768]{1,0:T(8,128)S(1)}) custom-call(s32[6]{0:T(128)S(1)} %copy-done.11, bf16[768,768]{1,0:T(8,128)(2,1)S(1)} %get-tuple-element.149.refs_5_.refs_4_.refs_1_, bf16[768,2304]{1,0:T(8,128)(2,1)S(1)} %get-tuple-element.127.refs_1_.refs_2_, f32[768,128]{1,0:T(8,128)S(1)} %get-tuple-element.150.refs_3_, ...), custom_call_target="tpu_custom_call" | custom-call | flops 30000001024 | bytes 30000000 | tf_op jit(solution)/shard_map/pallas_call | solution.py:69
  151.7 3.9 %shard_map.305 = (bf16[4,48,1920]{2,1,0:T(8,128)(2,1)S(1)}, bf16[4,48,1920]{2,1,0:T(8,128)(2,1)S(1)}, bf16[4,48,1920]{2,1,0:T(8,128)(2,1)S(1)}, bf16[2,48,1920]{...) custom-call(s32[1]{0:T(128)} %bitcast.3.refs_0_, s32[4]{0:T(128)S(1)} %pad_add_fusion.refs_0_.refs_1_, ...), custom_call_target="tpu_custom_call" | custom-call | flops 17200001024 | bytes 17200000 | tf_op jit(solution)/shard_map/pallas_call | solution.py:69
  157.1 7.8 %shard_map.306 = (bf16[768,2304]{1,0:T(8,128)(2,1)S(1)}, f32[16,768]{1,0:T(8,128)S(1)}) custom-call(s32[6]{0:T(128)S(1)} %copy-done.11, bf16[768,768]{1,0:T(8,128)(2,1)S(1)} %get-tuple-element.149.refs_5_.refs_4_.refs_1_, bf16[768,2304]{1,0:T(8,128)(2,1)S(1)} %get-tuple-element.127.refs_1_.refs_2_, f32[768,128]{1,0:T(8,128)S(1)} %get-tuple-element.150.refs_3_, ...), custom_call_target="tpu_custom_call" | custom-call | flops 30000001024 | bytes 30000000 | tf_op jit(solution)/shard_map/pallas_call | solution.py:69
  165.7 6.5 %shard_map.308 = (bf16[768,768]{1,0:T(8,128)(2,1)}, bf16[768,128]{1,0:T(8,128)(2,1)S(1)}, bf16[768,128]{1,0:T(8,128)(2,1)S(1)}, f32[8,128]{1,0:T(8,128)S(1)}) custom-call(s32[6]{0:T(128)S(1)} %copy-done.7, s32[4]{0:T(128)S(1)} %pad_add_fusion.refs_0_.refs_1_, bf16[768,2304]{1,0:T(8,128)(2,1)S(1)} %get-tuple-element.159.refs_4_.refs_2_.refs_3_, ...), custom_call_target="tpu_custom_call" | custom-call | flops 22799998976 | bytes 22800000 | tf_op jit(solution)/shard_map/pallas_call | solution.py:69
  181.8 5.6 %collective-permute-done.37.refs_4_ = bf16[2,192,384]{2,1,0:T(8,128)(2,1)S(1)} collective-permute-done((bf16[2,192,384]{2,1,0:T(8,128)(2,1)S(1)}, bf16[2,192,384]{2,1,0:T(8,128)(2,1)S(1)}, u32[]{:S(2)}, u32[]{:S(2)}) %collective-permute-start.37) | collective-permute-done | bytes 294944 | tf_op jit(solution)/shard_map/ppermute | solution.py:707
  192.7 3.4 %shard_map.312 = (bf16[4,48,1280]{2,1,0:T(8,128)(2,1)S(1)}, bf16[4,48,1280]{2,1,0:T(8,128)(2,1)S(1)}, bf16[4,48,1280]{2,1,0:T(8,128)(2,1)S(1)}, bf16[2,48,1280]{...) custom-call(s32[1]{0:T(128)} %bitcast.3.refs_0_, s32[4]{0:T(128)S(1)} %pad_add_fusion.refs_0_.refs_1_, ...), custom_call_target="tpu_custom_call" | custom-call | flops 17200001024 | bytes 17200000 | tf_op jit(solution)/shard_map/pallas_call | solution.py:69
  198.7 3.5 %collective-permute-done.42.refs_2_ = bf16[192,384]{1,0:T(8,128)(2,1)S(1)} collective-permute-done((bf16[192,384]{1,0:T(8,128)(2,1)S(1)}, bf16[192,384]{1,0:T(8,128)(2,1)S(1)}, u32[]{:S(2)}, u32[]{:S(2)}) %collective-permute-start.42) | collective-permute-done | bytes 147488 | tf_op jit(solution)/shard_map/ppermute | solution.py:710
  204.3 3.2 %collective-permute-start.57 = (bf16[48,1920]{1,0:T(8,128)(2,1)S(1)}, bf16[48,1920]{1,0:T(8,128)(2,1)S(1)}, u32[]{:S(2)}, u32[]{:S(2)}) collective-permute-start(bf16[48,1920]{1,0:T(8,128)(2,1)S(1)} %get-tuple-element.210), channel_id=1, source_target_pairs={{0,2},{1,3},{2,4},{3,5},{4,6},{5,7},{6,0},{7,1},{8,10},{9,11},{10,... | collective-permute-start | bytes 552968 | tf_op jit(solution)/shard_map/ppermute | solution.py:710
  207.6 2.6 %collective-permute-done.49.refs_3_ = bf16[192,384]{1,0:T(8,128)(2,1)S(1)} collective-permute-done((bf16[192,384]{1,0:T(8,128)(2,1)S(1)}, bf16[192,384]{1,0:T(8,128)(2,1)S(1)}, u32[]{:S(2)}, u32[]{:S(2)}) %collective-permute-start.49) | collective-permute-done | bytes 147488 | tf_op jit(solution)/shard_map/ppermute | solution.py:704
  210.7 3.1 %collective-permute-start.59 = (bf16[48,1920]{1,0:T(8,128)(2,1)S(1)}, bf16[48,1920]{1,0:T(8,128)(2,1)S(1)}, u32[]{:S(2)}, u32[]{:S(2)}) collective-permute-start(bf16[48,1920]{1,0:T(8,128)(2,1)S(1)} %get-tuple-element.212), channel_id=1, source_target_pairs={{0,6},{1,7},{2,0},{3,1},{4,2},{5,3},{6,4},{7,5},{8,14},{9,15},{10,... | collective-permute-start | bytes 552968 | tf_op jit(solution)/shard_map/ppermute | solution.py:710
  213.8 2.9 %collective-permute-start.50 = (bf16[192,384]{1,0:T(8,128)(2,1)S(1)}, bf16[192,384]{1,0:T(8,128)(2,1)S(1)}, u32[]{:S(2)}, u32[]{:S(2)}) collective-permute-start(bf16[192,384]{1,0:T(8,128)(2,1)S(1)} %collective-permute-done.49.refs_3_), channel_id=1, source_target_pairs={{0,8},{8,0},{16,24},{24,16},{1,9},{9,1},{17,25},{25,17},{2,10},{10... | collective-permute-start | bytes 442376 | tf_op jit(solution)/shard_map/ppermute | solution.py:701
  219.9 4.7 %collective-permute-done.46.refs_4_ = bf16[2,48,1280]{2,1,0:T(8,128)(2,1)S(1)} collective-permute-done((bf16[2,48,1280]{2,1,0:T(8,128)(2,1)S(1)}, bf16[2,48,1280]{2,1,0:T(8,128)(2,1)S(1)}, u32[]{:S(2)}, u32[]{:S(2)}) %collective-permute-start.46) | collective-permute-done | bytes 245792 | tf_op jit(solution)/shard_map/ppermute | solution.py:707
  229.8 2.0 collective-permute-start.60
  233.1 2.9 %collective-permute-done.52.refs_2_ = bf16[48,1280]{1,0:T(8,128)(2,1)S(1)} collective-permute-done((bf16[48,1280]{1,0:T(8,128)(2,1)S(1)}, bf16[48,1280]{1,0:T(8,128)(2,1)S(1)}, u32[]{:S(2)}, u32[]{:S(2)}) %collective-permute-start.52) | collective-permute-done | bytes 122912 | tf_op jit(solution)/shard_map/ppermute | solution.py:710
  237.7 3.7 %collective-permute-start.54 = (bf16[48,1280]{1,0:T(8,128)(2,1)S(1)}, bf16[48,1280]{1,0:T(8,128)(2,1)S(1)}, u32[]{:S(2)}, u32[]{:S(2)}) collective-permute-start(bf16[48,1280]{1,0:T(8,128)(2,1)S(1)} %get-tuple-element.206.refs_1_), channel_id=1, source_target_pairs={{0,8},{8,0},{16,24},{24,16},{1,9},{9,1},{17,25},{25,17},{2,10},{10... | collective-permute-start | bytes 368648 | tf_op jit(solution)/shard_map/ppermute | solution.py:701
  241.4 3.6 %collective-permute-start.56 = (bf16[48,1280]{1,0:T(8,128)(2,1)S(1)}, bf16[48,1280]{1,0:T(8,128)(2,1)S(1)}, u32[]{:S(2)}, u32[]{:S(2)}) collective-permute-start(bf16[48,1280]{1,0:T(8,128)(2,1)S(1)} %collective-permute-done.55.refs_3_), channel_id=1, source_target_pairs={{0,8},{8,0},{16,24},{24,16},{1,9},{9,1},{17,25},{25,17},{2,10},{10... | collective-permute-start | bytes 368648 | tf_op jit(solution)/shard_map/ppermute | solution.py:701
  (188 shorter events, 72.4 us)
Async XLA Ops:
  7.6 10.4 %collective-permute-start.1 = (bf16[48,1280]{1,0:T(8,128)(2,1)S(1)}, bf16[48,1280]{1,0:T(8,128)(2,1)S(1)}, u32[]{:S(2)}, u32[]{:S(2)}) collective-permute-start(bf16[48,1280]{1,0:T(8,128)(2,1)S(1)} %get-tuple-element.121.refs_1_), channel_id=1, source_target_pairs={{0,4},{1,5},{2,6},{3,7},{4,0},{5,1},{6,2},{7,3},{8,12},{9,13},{10,... | collective-permute-start | bytes 368648 | tf_op jit(solution)/shard_map/ppermute | solution.py:710
  18.5 19.3 %collective-permute-start.4 = (bf16[48,5120]{1,0:T(8,128)(2,1)S(1)}, bf16[48,5120]{1,0:T(8,128)(2,1)S(1)}, u32[]{:S(2)}, u32[]{:S(2)}) collective-permute-start(bf16[48,5120]{1,0:T(8,128)(2,1)S(1)} %shard_map.290.refs_1_), channel_id=1, source_target_pairs={{0,16},{8,24},{16,0},{24,8},{1,17},{9,25},{17,1},{25,9},{2,18},{10... | collective-permute-start | bytes 1474568 | tf_op jit(solution)/shard_map/ppermute | solution.py:704
  19.8 18.0 %collective-permute-start.3 = (bf16[48,5120]{1,0:T(8,128)(2,1)S(1)}, bf16[48,5120]{1,0:T(8,128)(2,1)S(1)}, u32[]{:S(2)}, u32[]{:S(2)}) collective-permute-start(bf16[48,5120]{1,0:T(8,128)(2,1)S(1)} %shard_map.290.refs_1_), channel_id=1, source_target_pairs={{0,1},{1,0},{2,3},{3,2},{4,5},{5,4},{6,7},{7,6},{8,9},{9,8},{10,11... | collective-permute-start | bytes 1474568 | tf_op jit(solution)/shard_map/ppermute | solution.py:707
  21.4 16.5 %collective-permute-start.6 = (bf16[48,1920]{1,0:T(8,128)(2,1)S(1)}, bf16[48,1920]{1,0:T(8,128)(2,1)S(1)}, u32[]{:S(2)}, u32[]{:S(2)}) collective-permute-start(bf16[48,1920]{1,0:T(8,128)(2,1)S(1)} %get-tuple-element.122.refs_4_.refs_1_), channel_id=1, source_target_pairs={{0,4},{1,5},{2,6},{3,7},{4,0},{5,1},{6,2},{7,3},{8,12},{9,13},{10,... | collective-permute-start | bytes 552968 | tf_op jit(solution)/shard_map/ppermute | solution.py:710
  23.2 14.7 %collective-permute-start.5 = (bf16[48,1920]{1,0:T(8,128)(2,1)S(1)}, bf16[48,1920]{1,0:T(8,128)(2,1)S(1)}, u32[]{:S(2)}, u32[]{:S(2)}) collective-permute-start(bf16[48,1920]{1,0:T(8,128)(2,1)S(1)} %get-tuple-element.122.refs_4_.refs_1_), channel_id=1, source_target_pairs={{0,2},{1,3},{2,4},{3,5},{4,6},{5,7},{6,0},{7,1},{8,10},{9,11},{10,... | collective-permute-start | bytes 552968 | tf_op jit(solution)/shard_map/ppermute | solution.py:710
  38.5 16.2 %collective-permute-start.8 = (bf16[48,15360]{1,0:T(8,128)(2,1)S(1)}, bf16[48,15360]{1,0:T(8,128)(2,1)S(1)}, u32[]{:S(2)}, u32[]{:S(2)}) collective-permute-start(bf16[48,15360]{1,0:T(8,128)(2,1)S(1)} %get-tuple-element.123.refs_4_), channel_id=1, source_target_pairs={{0,8},{8,0},{16,24},{24,16},{1,9},{9,1},{17,25},{25,17},{2,10},{10... | collective-permute-start | bytes 4423688 | tf_op jit(solution)/shard_map/ppermute | solution.py:701
  49.5 20.7 %collective-permute-start.14 = (bf16[48,7680]{1,0:T(8,128)(2,1)S(1)}, bf16[48,7680]{1,0:T(8,128)(2,1)S(1)}, u32[]{:S(2)}, u32[]{:S(2)}) collective-permute-start(bf16[48,7680]{1,0:T(8,128)(2,1)S(1)} %shard_map.292.refs_10_.refs_1_), channel_id=1, source_target_pairs={{0,16},{8,24},{16,0},{24,8},{1,17},{9,25},{17,1},{25,9},{2,18},{10... | collective-permute-start | bytes 2211848 | tf_op jit(solution)/shard_map/ppermute | solution.py:704
  49.8 20.4 %collective-permute-start.13 = (bf16[48,7680]{1,0:T(8,128)(2,1)S(1)}, bf16[48,7680]{1,0:T(8,128)(2,1)S(1)}, u32[]{:S(2)}, u32[]{:S(2)}) collective-permute-start(bf16[48,7680]{1,0:T(8,128)(2,1)S(1)} %shard_map.292.refs_10_.refs_1_), channel_id=1, source_target_pairs={{0,1},{1,0},{2,3},{3,2},{4,5},{5,4},{6,7},{7,6},{8,9},{9,8},{10,11... | collective-permute-start | bytes 2211848 | tf_op jit(solution)/shard_map/ppermute | solution.py:707
  53.8 16.3 %collective-permute-start.17 = (bf16[48,1536]{1,0:T(8,128)(2,1)S(1)}, bf16[48,1536]{1,0:T(8,128)(2,1)S(1)}, u32[]{:S(2)}, u32[]{:S(2)}) collective-permute-start(bf16[48,1536]{1,0:T(8,128)(2,1)S(1)} %get-tuple-element.130.refs_5_.refs_1_), channel_id=1, source_target_pairs={{0,6},{1,7},{2,0},{3,1},{4,2},{5,3},{6,4},{7,5},{8,14},{9,15},{10,... | collective-permute-start | bytes 442376 | tf_op jit(solution)/shard_map/ppermute | solution.py:710
  54.2 16.0 %collective-permute-start.16 = (bf16[48,1536]{1,0:T(8,128)(2,1)S(1)}, bf16[48,1536]{1,0:T(8,128)(2,1)S(1)}, u32[]{:S(2)}, u32[]{:S(2)}) collective-permute-start(bf16[48,1536]{1,0:T(8,128)(2,1)S(1)} %get-tuple-element.130.refs_5_.refs_1_), channel_id=1, source_target_pairs={{0,4},{1,5},{2,6},{3,7},{4,0},{5,1},{6,2},{7,3},{8,12},{9,13},{10,... | collective-permute-start | bytes 442376 | tf_op jit(solution)/shard_map/ppermute | solution.py:710
  54.8 15.4 %collective-permute-start.15 = (bf16[48,1536]{1,0:T(8,128)(2,1)S(1)}, bf16[48,1536]{1,0:T(8,128)(2,1)S(1)}, u32[]{:S(2)}, u32[]{:S(2)}) collective-permute-start(bf16[48,1536]{1,0:T(8,128)(2,1)S(1)} %get-tuple-element.130.refs_5_.refs_1_), channel_id=1, source_target_pairs={{0,2},{1,3},{2,4},{3,5},{4,6},{5,7},{6,0},{7,1},{8,10},{9,11},{10,... | collective-permute-start | bytes 442376 | tf_op jit(solution)/shard_map/ppermute | solution.py:710
  71.0 15.6 %collective-permute-start.18 = (bf16[48,23040]{1,0:T(8,128)(2,1)S(1)}, bf16[48,23040]{1,0:T(8,128)(2,1)S(1)}, u32[]{:S(2)}, u32[]{:S(2)}) collective-permute-start(bf16[48,23040]{1,0:T(8,128)(2,1)S(1)} %get-tuple-element.131.refs_7_), channel_id=1, source_target_pairs={{0,8},{8,0},{16,24},{24,16},{1,9},{9,1},{17,25},{25,17},{2,10},{10... | collective-permute-start | bytes 6635528 | tf_op jit(solution)/shard_map/ppermute | solution.py:701
  74.3 22.4 %collective-permute-start.24 = (bf16[48,6144]{1,0:T(8,128)(2,1)S(1)}, bf16[48,6144]{1,0:T(8,128)(2,1)S(1)}, u32[]{:S(2)}, u32[]{:S(2)}) collective-permute-start(bf16[48,6144]{1,0:T(8,128)(2,1)S(1)} %shard_map.296.refs_13_.refs_1_), channel_id=1, source_target_pairs={{0,16},{8,24},{16,0},{24,8},{1,17},{9,25},{17,1},{25,9},{2,18},{10... | collective-permute-start | bytes 1769480 | tf_op jit(solution)/shard_map/ppermute | solution.py:704
  74.6 22.1 %collective-permute-start.23 = (bf16[48,6144]{1,0:T(8,128)(2,1)S(1)}, bf16[48,6144]{1,0:T(8,128)(2,1)S(1)}, u32[]{:S(2)}, u32[]{:S(2)}) collective-permute-start(bf16[48,6144]{1,0:T(8,128)(2,1)S(1)} %shard_map.296.refs_13_.refs_1_), channel_id=1, source_target_pairs={{0,1},{1,0},{2,3},{3,2},{4,5},{5,4},{6,7},{7,6},{8,9},{9,8},{10,11... | collective-permute-start | bytes 1769480 | tf_op jit(solution)/shard_map/ppermute | solution.py:707
  97.5 13.8 %collective-permute-start.25 = (bf16[48,18432]{1,0:T(8,128)(2,1)S(1)}, bf16[48,18432]{1,0:T(8,128)(2,1)S(1)}, u32[]{:S(2)}, u32[]{:S(2)}) collective-permute-start(bf16[48,18432]{1,0:T(8,128)(2,1)S(1)} %get-tuple-element.142.refs_8_), channel_id=1, source_target_pairs={{0,8},{8,0},{16,24},{24,16},{1,9},{9,1},{17,25},{25,17},{2,10},{10... | collective-permute-start | bytes 5308424 | tf_op jit(solution)/shard_map/ppermute | solution.py:701
  142.8 22.2 %collective-permute-start.32 = (bf16[4,192,384]{2,1,0:T(8,128)(2,1)S(1)}, bf16[4,192,384]{2,1,0:T(8,128)(2,1)S(1)}, u32[]{:S(2)}, u32[]{:S(2)}) collective-permute-start(bf16[4,192,384]{2,1,0:T(8,128)(2,1)S(1)} %get-tuple-element.163), channel_id=1, source_target_pairs={{0,1},{1,0},{2,3},{3,2},{4,5},{5,4},{6,7},{7,6},{8,9},{9,8},{10,11... | collective-permute-start | bytes 1769480 | tf_op jit(solution)/shard_map/ppermute | solution.py:707
  143.0 21.9 %collective-permute-start.33 = (bf16[4,192,384]{2,1,0:T(8,128)(2,1)S(1)}, bf16[4,192,384]{2,1,0:T(8,128)(2,1)S(1)}, u32[]{:S(2)}, u32[]{:S(2)}) collective-permute-start(bf16[4,192,384]{2,1,0:T(8,128)(2,1)S(1)} %get-tuple-element.164), channel_id=1, source_target_pairs={{0,16},{8,24},{16,0},{24,8},{1,17},{9,25},{17,1},{25,9},{2,18},{10... | collective-permute-start | bytes 1769480 | tf_op jit(solution)/shard_map/ppermute | solution.py:704
  155.7 17.5 %collective-permute-start.34 = (bf16[4,48,1920]{2,1,0:T(8,128)(2,1)S(1)}, bf16[4,48,1920]{2,1,0:T(8,128)(2,1)S(1)}, u32[]{:S(2)}, u32[]{:S(2)}) collective-permute-start(bf16[4,48,1920]{2,1,0:T(8,128)(2,1)S(1)} %get-tuple-element.171), channel_id=1, source_target_pairs={{0,1},{1,0},{2,3},{3,2},{4,5},{5,4},{6,7},{7,6},{8,9},{9,8},{10,11... | collective-permute-start | bytes 2211848 | tf_op jit(solution)/shard_map/ppermute | solution.py:707
  156.9 17.1 %collective-permute-start.35 = (bf16[4,48,1920]{2,1,0:T(8,128)(2,1)S(1)}, bf16[4,48,1920]{2,1,0:T(8,128)(2,1)S(1)}, u32[]{:S(2)}, u32[]{:S(2)}) collective-permute-start(bf16[4,48,1920]{2,1,0:T(8,128)(2,1)S(1)} %get-tuple-element.172), channel_id=1, source_target_pairs={{0,16},{8,24},{16,0},{24,8},{1,17},{9,25},{17,1},{25,9},{2,18},{10... | collective-permute-start | bytes 2211848 | tf_op jit(solution)/shard_map/ppermute | solution.py:704
  177.0 14.1 %collective-permute-start.36 = (bf16[768,1280]{1,0:T(8,128)(2,1)S(1)}, bf16[768,1280]{1,0:T(8,128)(2,1)S(1)}, u32[]{:S(2)}, u32[]{:S(2)}) collective-permute-start(bf16[768,1280]{1,0:T(8,128)(2,1)S(1)} %shard_map.310.refs_6_), channel_id=1, source_target_pairs={{0,8},{8,0},{16,24},{24,16},{1,9},{9,1},{17,25},{25,17},{2,10},{10... | collective-permute-start | bytes 5898248 | tf_op jit(solution)/shard_map/ppermute | solution.py:701
  180.1 16.1 %collective-permute-start.44 = (bf16[2,48,1920]{2,1,0:T(8,128)(2,1)S(1)}, bf16[2,48,1920]{2,1,0:T(8,128)(2,1)S(1)}, u32[]{:S(2)}, u32[]{:S(2)}) collective-permute-start(bf16[2,48,1920]{2,1,0:T(8,128)(2,1)S(1)} %get-tuple-element.192), channel_id=1, source_target_pairs={{0,1},{1,0},{2,3},{3,2},{4,5},{5,4},{6,7},{7,6},{8,9},{9,8},{10,11... | collective-permute-start | bytes 1105928 | tf_op jit(solution)/shard_map/ppermute | solution.py:707
  180.6 16.8 %collective-permute-start.45 = (bf16[2,48,1920]{2,1,0:T(8,128)(2,1)S(1)}, bf16[2,48,1920]{2,1,0:T(8,128)(2,1)S(1)}, u32[]{:S(2)}, u32[]{:S(2)}) collective-permute-start(bf16[2,48,1920]{2,1,0:T(8,128)(2,1)S(1)} %get-tuple-element.193), channel_id=1, source_target_pairs={{0,16},{8,24},{16,0},{24,8},{1,17},{9,25},{17,1},{25,9},{2,18},{10... | collective-permute-start | bytes 1105928 | tf_op jit(solution)/shard_map/ppermute | solution.py:704
  189.3 12.9 %collective-permute-start.42 = (bf16[192,384]{1,0:T(8,128)(2,1)S(1)}, bf16[192,384]{1,0:T(8,128)(2,1)S(1)}, u32[]{:S(2)}, u32[]{:S(2)}) collective-permute-start(bf16[192,384]{1,0:T(8,128)(2,1)S(1)} %get-tuple-element.189), channel_id=1, source_target_pairs={{0,4},{1,5},{2,6},{3,7},{4,0},{5,1},{6,2},{7,3},{8,12},{9,13},{10,... | collective-permute-start | bytes 442376 | tf_op jit(solution)/shard_map/ppermute | solution.py:710
  191.1 11.1 %collective-permute-start.43 = (bf16[192,384]{1,0:T(8,128)(2,1)S(1)}, bf16[192,384]{1,0:T(8,128)(2,1)S(1)}, u32[]{:S(2)}, u32[]{:S(2)}) collective-permute-start(bf16[192,384]{1,0:T(8,128)(2,1)S(1)} %get-tuple-element.190), channel_id=1, source_target_pairs={{0,6},{1,7},{2,0},{3,1},{4,2},{5,3},{6,4},{7,5},{8,14},{9,15},{10,... | collective-permute-start | bytes 442376 | tf_op jit(solution)/shard_map/ppermute | solution.py:710
  196.2 14.5 %collective-permute-start.39 = (bf16[4,48,1280]{2,1,0:T(8,128)(2,1)S(1)}, bf16[4,48,1280]{2,1,0:T(8,128)(2,1)S(1)}, u32[]{:S(2)}, u32[]{:S(2)}) collective-permute-start(bf16[4,48,1280]{2,1,0:T(8,128)(2,1)S(1)} %get-tuple-element.183), channel_id=1, source_target_pairs={{0,1},{1,0},{2,3},{3,2},{4,5},{5,4},{6,7},{7,6},{8,9},{9,8},{10,11... | collective-permute-start | bytes 1474568 | tf_op jit(solution)/shard_map/ppermute | solution.py:707
  197.4 16.5 %collective-permute-start.40 = (bf16[4,48,1280]{2,1,0:T(8,128)(2,1)S(1)}, bf16[4,48,1280]{2,1,0:T(8,128)(2,1)S(1)}, u32[]{:S(2)}, u32[]{:S(2)}) collective-permute-start(bf16[4,48,1280]{2,1,0:T(8,128)(2,1)S(1)} %get-tuple-element.184), channel_id=1, source_target_pairs={{0,16},{8,24},{16,0},{24,8},{1,17},{9,25},{17,1},{25,9},{2,18},{10... | collective-permute-start | bytes 1474568 | tf_op jit(solution)/shard_map/ppermute | solution.py:704
  203.3 13.6 %collective-permute-start.48 = (bf16[192,384]{1,0:T(8,128)(2,1)S(1)}, bf16[192,384]{1,0:T(8,128)(2,1)S(1)}, u32[]{:S(2)}, u32[]{:S(2)}) collective-permute-start(bf16[192,384]{1,0:T(8,128)(2,1)S(1)} %get-tuple-element.199.refs_1_), channel_id=1, source_target_pairs={{0,8},{8,0},{16,24},{24,16},{1,9},{9,1},{17,25},{25,17},{2,10},{10... | collective-permute-start | bytes 442376 | tf_op jit(solution)/shard_map/ppermute | solution.py:701
  204.3 21.5 %collective-permute-start.57 = (bf16[48,1920]{1,0:T(8,128)(2,1)S(1)}, bf16[48,1920]{1,0:T(8,128)(2,1)S(1)}, u32[]{:S(2)}, u32[]{:S(2)}) collective-permute-start(bf16[48,1920]{1,0:T(8,128)(2,1)S(1)} %get-tuple-element.210), channel_id=1, source_target_pairs={{0,2},{1,3},{2,4},{3,5},{4,6},{5,7},{6,0},{7,1},{8,10},{9,11},{10,... | collective-permute-start | bytes 552968 | tf_op jit(solution)/shard_map/ppermute | solution.py:710
  210.2 15.6 %collective-permute-start.58 = (bf16[48,1920]{1,0:T(8,128)(2,1)S(1)}, bf16[48,1920]{1,0:T(8,128)(2,1)S(1)}, u32[]{:S(2)}, u32[]{:S(2)}) collective-permute-start(bf16[48,1920]{1,0:T(8,128)(2,1)S(1)} %get-tuple-element.211), channel_id=1, source_target_pairs={{0,4},{1,5},{2,6},{3,7},{4,0},{5,1},{6,2},{7,3},{8,12},{9,13},{10,... | collective-permute-start | bytes 552968 | tf_op jit(solution)/shard_map/ppermute | solution.py:710
  210.7 15.1 %collective-permute-start.59 = (bf16[48,1920]{1,0:T(8,128)(2,1)S(1)}, bf16[48,1920]{1,0:T(8,128)(2,1)S(1)}, u32[]{:S(2)}, u32[]{:S(2)}) collective-permute-start(bf16[48,1920]{1,0:T(8,128)(2,1)S(1)} %get-tuple-element.212), channel_id=1, source_target_pairs={{0,6},{1,7},{2,0},{3,1},{4,2},{5,3},{6,4},{7,5},{8,14},{9,15},{10,... | collective-permute-start | bytes 552968 | tf_op jit(solution)/shard_map/ppermute | solution.py:710
  229.8 15.2 %collective-permute-start.60 = (bf16[48,1920]{1,0:T(8,128)(2,1)S(1)}, bf16[48,1920]{1,0:T(8,128)(2,1)S(1)}, u32[]{:S(2)}, u32[]{:S(2)}) collective-permute-start(bf16[48,1920]{1,0:T(8,128)(2,1)S(1)} %get-tuple-element.214.refs_1_), channel_id=1, source_target_pairs={{0,8},{8,0},{16,24},{24,16},{1,9},{9,1},{17,25},{25,17},{2,10},{10... | collective-permute-start | bytes 552968 | tf_op jit(solution)/shard_map/ppermute | solution.py:701
  231.7 13.3 %collective-permute-start.62 = (bf16[48,1920]{1,0:T(8,128)(2,1)S(1)}, bf16[48,1920]{1,0:T(8,128)(2,1)S(1)}, u32[]{:S(2)}, u32[]{:S(2)}) collective-permute-start(bf16[48,1920]{1,0:T(8,128)(2,1)S(1)} %collective-permute-done.61.refs_3_), channel_id=1, source_target_pairs={{0,8},{8,0},{16,24},{24,16},{1,9},{9,1},{17,25},{25,17},{2,10},{10... | collective-permute-start | bytes 552968 | tf_op jit(solution)/shard_map/ppermute | solution.py:701
  (59 other events, 463.8 us)
where the time goes:
time: 254 us; the launch traced here: 249 us
  Pallas kernels  102 us (40%)
  starting transfers between devices  70.2 us (28%)
  waiting for transfers between devices  69.7 us (27%)
  local copies, waits for them, and re-layouts  4.48 us (2%)
    pallas_call x33, Pallas kernels, call(): pl.pallas_call(run, grid_spec=pltpu.PrefetchScalarGridSpec(num_scalar_pre...  102 us
    ppermute x18, waiting for transfers between devices, shift(): lax.ppermute(value, 'fsdp', [(f, (f + step * XS) % self.shards) for f in...  29.8 us
    ppermute x18, starting transfers between devices, core(): return lax.ppermute(value, 'rep', [(r, r ^ 1) for r in range(self.reps)])  27.4 us
    ppermute x18, starting transfers between devices, shift(): lax.ppermute(value, 'fsdp', [(f, (f + step * XS) % self.shards) for f in...  24.3 us
    ppermute x15, waiting for transfers between devices, y(): return lax.ppermute(value, 'rep', [(r, r ^ 2) for r in range(self.reps)])  18.5 us
    ppermute x12, waiting for transfers between devices, x(): return lax.ppermute(value, 'fsdp', [(f, f ^ 1) for f in range(self.shards)])  18.3 us
    ppermute x15, starting transfers between devices, y(): return lax.ppermute(value, 'rep', [(r, r ^ 2) for r in range(self.reps)])  10.2 us
    ppermute x12, starting transfers between devices, x(): return lax.ppermute(value, 'fsdp', [(f, f ^ 1) for f in range(self.shards)])  8.26 us
  transfers between devices with their start and end apart: 63, of which 20 were waited for; matrix products, arithmetic and copies ran while one was open for 0% of the time, Pallas kernels for 28%

commit v1 on v0

--- a/solution.py
+++ b/solution.py
@@ -163,32 +163,26 @@
     return kinds, spots
 
 
-def selector(width, shards):
-    each = width // shards
-    row = lax.broadcasted_iota(jnp.int32, (width, shards * TFREQ), 0)
-    column = lax.broadcasted_iota(jnp.int32, (width, shards * TFREQ), 1)
-    lane = column % TFREQ
-    return ((row == (column // TFREQ) * each + lane) & (lane < each)).astype(HALF)
-
-
 def kind_rows(kinds, shards):
     return (kinds == lax.broadcasted_iota(jnp.int32, (TALL * shards, TALL), 1)).astype(HALF)
 
 
 def table_of(pieces, width, shards):
     kinds, spots = vector_map(shards)
-    wide = jnp.concatenate([jnp.where(spots == m, pieces, jnp.zeros_like(pieces)) for m in range(shards)], axis=1)
-    spread = dot(wide, selector(width, shards), (1, 1)).astype(HALF)
-    return dot(kind_rows(kinds, shards), spread, (0, 0))
+    values = pieces.astype(WIDE)[:, : width // shards]
+    spread = jnp.concatenate([jnp.where(spots == m, values, 0.0) for m in range(shards)], axis=1)
+    return dot(kind_rows(kinds, shards), spread.astype(HALF), (0, 0))
 
 
 def pieces_of(table, width, shards):
     kinds, spots = vector_map(shards)
-    spread = dot(dot(kind_rows(kinds, shards), table).astype(HALF), selector(width, shards))
-    out = jnp.zeros((TALL * shards, TFREQ), WIDE)
+    each = width // shards
+    spread = dot(kind_rows(kinds, shards), table)
+    out = jnp.zeros((TALL * shards, each), WIDE)
     for m in range(shards):
-        out = jnp.where(spots == m, spread[:, m * TFREQ : (m + 1) * TFREQ], out)
-    return out.astype(HALF)
+        out = jnp.where(spots == m, spread[:, m * each : (m + 1) * each], out)
+    blank = jnp.zeros((TALL * shards, TFREQ - each), WIDE)
+    return jnp.concatenate([out, blank], axis=1).astype(HALF)
 
 
 def add_time(start_of, bounds_ref, temb, seqs, span, use):
@@ -1094,11 +1088,9 @@
     if by_hand:
         state2 = second_hop(first_hop(kept2, routes), routes, after=[done])
         sent = outer(away, [(start_b, dproj)], more[0], after=[state2[-1]])
-        terms3 = line_sum(spot, state3, after=[sent])
-        kept1 = keep_outer(
-            mine, spot, [(start_b, dproj)], routes.core(sent), zs, extras, after=[terms3[-1]]
-        )
-        terms2 = line_sum(spot, state2, after=[kept1[-1]])
+        kept1 = keep_outer(mine, spot, [(start_b, dproj)], routes.core(sent), zs, extras, after=[state2[-1]])
+        terms3 = line_sum(spot, state3, after=[kept1[-1]])
+        terms2 = line_sum(spot, state2, after=[terms3[-1]])
         sums3, token = last_hops(terms3, routes, after=[terms2[-1]])
         state1 = second_hop(first_hop(kept1, routes), routes, after=[token])
         out_down, token = finish(
@@ -1121,6 +1113,7 @@
             [(c, 0, half, 0, c * half) for c in range(2)] + [(0, half, TFREQ, 1, 0)],
             [weight_qkv.shape, weight_time.shape],
             (part, [v.shape[0] for v in small]),
+            after=[token],
         )
     else:
 

time: 254 us -> 252 us (level)
  transfers between devices with their start and end apart: 63 -> 63, of which waited for: 20 -> 21; matrix products, arithmetic and copies ran while one was open for 0% -> 0% of each run, Pallas kernels for 28% -> 28%
where the time goes in v1:
time: 252 us; the launch traced here: 247 us
  Pallas kernels  101 us (40%)
  waiting for transfers between devices  70.3 us (28%)
  starting transfers between devices  68.9 us (27%)
  local copies, waits for them, and re-layouts  4.48 us (2%)
    pallas_call x33, Pallas kernels, call(): pl.pallas_call(run, grid_spec=pltpu.PrefetchScalarGridSpec(num_scalar_pre...  101 us
    ppermute x18, waiting for transfers between devices, shift(): lax.ppermute(value, 'fsdp', [(f, (f + step * XS) % self.shards) for f in...  29.7 us
    ppermute x18, starting transfers between devices, core(): return lax.ppermute(value, 'rep', [(r, r ^ 1) for r in range(self.reps)])  26.6 us
    ppermute x18, starting transfers between devices, shift(): lax.ppermute(value, 'fsdp', [(f, (f + step * XS) % self.shards) for f in...  23.3 us
    ppermute x15, waiting for transfers between devices, y(): return lax.ppermute(value, 'rep', [(r, r ^ 2) for r in range(self.reps)])  19.9 us
    ppermute x12, waiting for transfers between devices, x(): return lax.ppermute(value, 'fsdp', [(f, f ^ 1) for f in range(self.shards)])  16.5 us
    ppermute x15, starting transfers between devices, y(): return lax.ppermute(value, 'rep', [(r, r ^ 2) for r in range(self.reps)])  10.9 us
    ppermute x12, starting transfers between devices, x(): return lax.ppermute(value, 'fsdp', [(f, f ^ 1) for f in range(self.shards)])  8.09 us
  transfers between devices with their start and end apart: 63, of which 21 were waited for; matrix products, arithmetic and copies ran while one was open for 0% of the time, Pallas kernels for 28%

profile of v1, /device:TPU:1, one launch (start us, length us, event | category | flops | bytes accessed | tf_op | source)
XLA Modules:
  0.0 247.1 jit_solution(17451126691019242425)
XLA Ops:
  0.8 2.6 %shard_map.289 = (bf16[48,1280]{1,0:T(8,128)(2,1)S(1)}, bf16[48,1920]{1,0:T(8,128)(2,1)S(1)}, bf16[48,1536]{1,0:T(8,128)(2,1)S(1)}) custom-call(s32[4]{0:T(128)S(1)} %pad_add_fusion.refs_0_.refs_1_, bf16[96,2304]{1,0:T(8,128)(2,1)} %refs_1_.4, bf16[96,128]{1,0:T(8,128)(2,1)} %refs_2_.3, bf16[96,3072]{1,0:T(8,128)(2,1)} %refs_3_.1, bf16[96,768]{1,0:T(8,128)(2,1)} %refs_4_.1, ...), custom_call_target="tpu_custom_call" | custom-call | flops 750000000 | bytes 750000 | tf_op jit(solution)/shard_map/pallas_call | solution.py:69
  3.3 4.2 %collective-permute-start.2 = (bf16[48,1280]{1,0:T(8,128)(2,1)S(1)}, bf16[48,1280]{1,0:T(8,128)(2,1)S(1)}, u32[]{:S(2)}, u32[]{:S(2)}) collective-permute-start(bf16[48,1280]{1,0:T(8,128)(2,1)S(1)} %get-tuple-element.122.refs_1_), channel_id=1, source_target_pairs={{0,6},{1,7},{2,0},{3,1},{4,2},{5,3},{6,4},{7,5},{8,14},{9,15},{10,... | collective-permute-start | bytes 368648 | tf_op jit(solution)/shard_map/ppermute | solution.py:704
  9.4 8.5 %collective-permute-done.1.refs_3_ = bf16[48,1280]{1,0:T(8,128)(2,1)S(1)} collective-permute-done((bf16[48,1280]{1,0:T(8,128)(2,1)S(1)}, bf16[48,1280]{1,0:T(8,128)(2,1)S(1)}, u32[]{:S(2)}, u32[]{:S(2)}) %collective-permute-start.1) | collective-permute-done | bytes 122912 | tf_op jit(solution)/shard_map/ppermute | solution.py:704
  25.7 12.1 %collective-permute-done.6.refs_6_.refs_3_ = bf16[48,1920]{1,0:T(8,128)(2,1)S(1)} collective-permute-done((bf16[48,1920]{1,0:T(8,128)(2,1)S(1)}, bf16[48,1920]{1,0:T(8,128)(2,1)S(1)}, u32[]{:S(2)}, u32[]{:S(2)}) %collective-permute-start.6) | collective-permute-done | bytes 184352 | tf_op jit(solution)/shard_map/ppermute | solution.py:704
  38.5 2.8 %collective-permute-start.8 = (bf16[48,15360]{1,0:T(8,128)(2,1)S(1)}, bf16[48,15360]{1,0:T(8,128)(2,1)S(1)}, u32[]{:S(2)}, u32[]{:S(2)}) collective-permute-start(bf16[48,15360]{1,0:T(8,128)(2,1)S(1)} %get-tuple-element.124.refs_4_), channel_id=1, source_target_pairs={{0,8},{8,0},{16,24},{24,16},{1,9},{9,1},{17,25},{25,17},{2,10},{10... | collective-permute-start | bytes 4423688 | tf_op jit(solution)/shard_map/ppermute | solution.py:695
  41.9 7.0 %collective-permute-done.9.refs_5_.refs_6_ = bf16[48,2560]{1,0:T(8,128)(2,1)S(1)} collective-permute-done((bf16[48,2560]{1,0:T(8,128)(2,1)S(1)}, bf16[48,2560]{1,0:T(8,128)(2,1)S(1)}, u32[]{:S(2)}, u32[]{:S(2)}) %collective-permute-start.9) | collective-permute-done | bytes 245792 | tf_op jit(solution)/shard_map/ppermute | solution.py:701
  55.9 6.3 %shard_map.293 = (bf16[768,768]{1,0:T(8,128)(2,1)S(1)}, bf16[768,2304]{1,0:T(8,128)(2,1)S(1)}, f32[16,768]{1,0:T(8,128)S(1)}, bf16[768,128]{1,0:T(8,128)(2,1)S(1)}, bf16[4,2,2,48,2560]{4,3,2,1,0:T(8,128)(2,1)S(1)}) custom-call(s32[4]{0:T(128)S(1)} %pad_add_fusion.refs_0_.refs_1_, s32[6]{0:T(128)S(1)} %copy-done.6, bf16[768,768]{1,0:T(8,128)(2,1)S(1)} %copy-done.1, ...), custom_call_target="tpu_custom_call" | custom-call | flops 1750000000 | bytes 1750000 | tf_op jit(solution)/shard_map/pallas_call | solution.py:69
  62.3 7.2 %shard_map.294 = (bf16[768,768]{1,0:T(8,128)(2,1)S(1)}, f32[768,128]{1,0:T(8,128)S(1)}) custom-call(s32[6]{0:T(128)S(1)} %copy-done.11, bf16[768,2304]{1,0:T(8,128)(2,1)S(1)} %get-tuple-element.128.refs_1_.refs_2_), custom_call_target="tpu_custom_call" | custom-call | flops 1750000000 | bytes 1750000 | tf_op jit(solution)/shard_map/pallas_call | solution.py:69
  75.1 6.6 %collective-permute-done.21.refs_11_ = bf16[48,3840]{1,0:T(8,128)(2,1)S(1)} collective-permute-done((bf16[48,3840]{1,0:T(8,128)(2,1)S(1)}, bf16[48,3840]{1,0:T(8,128)(2,1)S(1)}, u32[]{:S(2)}, u32[]{:S(2)}) %collective-permute-start.21) | collective-permute-done | bytes 368672 | tf_op jit(solution)/shard_map/ppermute | solution.py:698
  87.4 8.7 %shard_map.297 = (f32[768,768]{1,0:T(8,128)S(1)}, bf16[768,768]{1,0:T(8,128)(2,1)S(1)}, f32[768,128]{1,0:T(8,128)S(1)}, bf16[768,3072]{1,0:T(8,128)(2,1)S(1)}, b...) custom-call(s32[4]{0:T(128)S(1)} %pad_add_fusion.refs_0_.refs_1_, ...), custom_call_target="tpu_custom_call" | custom-call | flops 2175000064 | bytes 2175000 | tf_op jit(solution)/shard_map/pallas_call | solution.py:69
  97.7 8.0 %collective-permute-done.28.refs_12_ = bf16[48,3072]{1,0:T(8,128)(2,1)S(1)} collective-permute-done((bf16[48,3072]{1,0:T(8,128)(2,1)S(1)}, bf16[48,3072]{1,0:T(8,128)(2,1)S(1)}, u32[]{:S(2)}, u32[]{:S(2)}) %collective-permute-start.28) | collective-permute-done | bytes 294944 | tf_op jit(solution)/shard_map/ppermute | solution.py:698
  106.9 3.6 %shard_map.299 = (bf16[768,3072]{1,0:T(8,128)(2,1)S(1)}, bf16[768,3072]{1,0:T(8,128)(2,1)S(1)}) custom-call(bf16[768,768]{1,0:T(8,128)(2,1)S(1)} %get-tuple-element.135.refs_4_.refs_0_.refs_1_.refs_2_, f32[16,768]{1,0:T(8,128)S(1)} %get-tuple-element.130.refs_6_.refs_1_.refs_7_.refs_4_, ...), custom_call_target="tpu_custom_call", output_to_operand_aliasing={{0}: (3, {}), {1}: (4, {})} | custom-call | flops 925000000 | bytes 925000 | tf_op jit(solution)/shard_map/pallas_call | solution.py:69
  112.0 17.9 %shard_map.300 = (bf16[768,768]{1,0:T(8,128)(2,1)}, f32[768,768]{1,0:T(8,128)S(1)}, bf16[768,768]{1,0:T(8,128)(2,1)S(1)}, bf16[768,3072]{1,0:T(8,128)(2,1)S(1)},...) custom-call(s32[4]{0:T(128)S(1)} %pad_add_fusion.refs_0_.refs_1_, s32[6]{0:T(128)S(1)} %copy-done.11, ...), custom_call_target="tpu_custom_call" | custom-call | flops 70799998976 | bytes 70800000 | tf_op jit(solution)/shard_map/pallas_call | solution.py:69
  130.3 5.2 %shard_map.301 = (f32[768,768]{1,0:T(8,128)S(1)}, bf16[768,768]{1,0:T(8,128)(2,1)S(1)}, f32[16,768]{1,0:T(8,128)S(1)}) custom-call(bf16[768,3072]{1,0:T(8,128)(2,1)S(1)} %get-tuple-element.146.refs_0_.refs_2_.refs_3_, f32[768,768]{1,0:T(8,128)S(1)} %get-tuple-element.147.refs_1_, f32[768,768]{1,0:T(8,128)S(1)} %get-tuple-element.142.refs_5_.refs_2_, ...), custom_call_target="tpu_custom_call" | custom-call | flops 20400001024 | bytes 20400000 | tf_op jit(solution)/shard_map/pallas_call | solution.py:69
  135.5 3.6 %shard_map.302 = (bf16[4,192,384]{2,1,0:T(8,128)(2,1)S(1)}, bf16[4,192,384]{2,1,0:T(8,128)(2,1)S(1)}, bf16[4,192,384]{2,1,0:T(8,128)(2,1)S(1)}, bf16[2,192,384]{...) custom-call(s32[1]{0:T(128)} %bitcast.3.refs_0_, s32[4]{0:T(128)S(1)} %pad_add_fusion.refs_0_.refs_1_, ...), custom_call_target="tpu_custom_call" | custom-call | flops 17200001024 | bytes 17200000 | tf_op jit(solution)/shard_map/pallas_call | solution.py:69
  139.1 2.6 %shard_map.303.refs_6_ = bf16[768,1920]{1,0:T(8,128)(2,1)S(1)} custom-call(s32[1]{0:T(128)S(6)} %sub.12.refs_2_.refs_0_, bf16[768,768]{1,0:T(8,128)(2,1)S(1)} %get-tuple-element.135.refs_4_.refs_0_.refs_1_.refs_2_, bf16[768,3072]{1,0:T(8,128)(2,1)S(1)} %get-tuple-element.146.refs_0_.refs_2_.refs_3_, ...), custom_call_target="tpu_custom_call" | custom-call | flops 11200000000 | bytes 11200000 | tf_op jit(solution)/shard_map/pallas_call | solution.py:69
  143.6 7.4 %shard_map.304 = (bf16[384,2304]{1,0:T(8,128)(2,1)S(1)}, f32[16,768]{1,0:T(8,128)S(1)}) custom-call(s32[6]{0:T(128)S(1)} %copy-done.11, bf16[768,768]{1,0:T(8,128)(2,1)S(1)} %get-tuple-element.150.refs_5_.refs_4_.refs_1_, bf16[768,2304]{1,0:T(8,128)(2,1)S(1)} %get-tuple-element.128.refs_1_.refs_2_, f32[768,128]{1,0:T(8,128)S(1)} %get-tuple-element.151.refs_3_, ...), custom_call_target="tpu_custom_call" | custom-call | flops 30000001024 | bytes 30000000 | tf_op jit(solution)/shard_map/pallas_call | solution.py:69
  151.0 3.9 %shard_map.305 = (bf16[4,48,1920]{2,1,0:T(8,128)(2,1)S(1)}, bf16[4,48,1920]{2,1,0:T(8,128)(2,1)S(1)}, bf16[4,48,1920]{2,1,0:T(8,128)(2,1)S(1)}, bf16[2,48,1920]{...) custom-call(s32[1]{0:T(128)} %bitcast.3.refs_0_, s32[4]{0:T(128)S(1)} %pad_add_fusion.refs_0_.refs_1_, ...), custom_call_target="tpu_custom_call" | custom-call | flops 17200001024 | bytes 17200000 | tf_op jit(solution)/shard_map/pallas_call | solution.py:69
  156.4 7.8 %shard_map.306 = (bf16[768,2304]{1,0:T(8,128)(2,1)S(1)}, f32[16,768]{1,0:T(8,128)S(1)}) custom-call(s32[6]{0:T(128)S(1)} %copy-done.11, bf16[768,768]{1,0:T(8,128)(2,1)S(1)} %get-tuple-element.150.refs_5_.refs_4_.refs_1_, bf16[768,2304]{1,0:T(8,128)(2,1)S(1)} %get-tuple-element.128.refs_1_.refs_2_, f32[768,128]{1,0:T(8,128)S(1)} %get-tuple-element.151.refs_3_, ...), custom_call_target="tpu_custom_call" | custom-call | flops 30000001024 | bytes 30000000 | tf_op jit(solution)/shard_map/pallas_call | solution.py:69
  164.9 6.2 %shard_map.308 = (bf16[768,768]{1,0:T(8,128)(2,1)}, bf16[768,128]{1,0:T(8,128)(2,1)S(1)}, bf16[768,128]{1,0:T(8,128)(2,1)S(1)}, f32[8,128]{1,0:T(8,128)S(1)}) custom-call(s32[6]{0:T(128)S(1)} %copy-done.7, s32[4]{0:T(128)S(1)} %pad_add_fusion.refs_0_.refs_1_, bf16[768,2304]{1,0:T(8,128)(2,1)S(1)} %get-tuple-element.160.refs_4_.refs_2_.refs_3_, ...), custom_call_target="tpu_custom_call" | custom-call | flops 22799998976 | bytes 22800000 | tf_op jit(solution)/shard_map/pallas_call | solution.py:69
  181.8 3.4 %shard_map.311 = (bf16[4,48,1280]{2,1,0:T(8,128)(2,1)S(1)}, bf16[4,48,1280]{2,1,0:T(8,128)(2,1)S(1)}, bf16[4,48,1280]{2,1,0:T(8,128)(2,1)S(1)}, bf16[2,48,1280]{...) custom-call(s32[1]{0:T(128)} %bitcast.3.refs_0_, s32[4]{0:T(128)S(1)} %pad_add_fusion.refs_0_.refs_1_, ...), custom_call_target="tpu_custom_call" | custom-call | flops 17200001024 | bytes 17200000 | tf_op jit(solution)/shard_map/pallas_call | solution.py:69
  192.0 2.7 %collective-permute-done.44.refs_4_ = bf16[2,48,1920]{2,1,0:T(8,128)(2,1)S(1)} collective-permute-done((bf16[2,48,1920]{2,1,0:T(8,128)(2,1)S(1)}, bf16[2,48,1920]{2,1,0:T(8,128)(2,1)S(1)}, u32[]{:S(2)}, u32[]{:S(2)}) %collective-permute-start.44) | collective-permute-done | bytes 368672 | tf_op jit(solution)/shard_map/ppermute | solution.py:701
  197.0 4.5 %collective-permute-done.42.refs_2_ = bf16[192,384]{1,0:T(8,128)(2,1)S(1)} collective-permute-done((bf16[192,384]{1,0:T(8,128)(2,1)S(1)}, bf16[192,384]{1,0:T(8,128)(2,1)S(1)}, u32[]{:S(2)}, u32[]{:S(2)}) %collective-permute-start.42) | collective-permute-done | bytes 147488 | tf_op jit(solution)/shard_map/ppermute | solution.py:704
  202.5 3.4 %collective-permute-start.57 = (bf16[48,1920]{1,0:T(8,128)(2,1)S(1)}, bf16[48,1920]{1,0:T(8,128)(2,1)S(1)}, u32[]{:S(2)}, u32[]{:S(2)}) collective-permute-start(bf16[48,1920]{1,0:T(8,128)(2,1)S(1)} %get-tuple-element.209), channel_id=1, source_target_pairs={{0,2},{1,3},{2,4},{3,5},{4,6},{5,7},{6,0},{7,1},{8,10},{9,11},{10,... | collective-permute-start | bytes 552968 | tf_op jit(solution)/shard_map/ppermute | solution.py:704
  206.0 3.5 %collective-permute-done.49.refs_3_ = bf16[192,384]{1,0:T(8,128)(2,1)S(1)} collective-permute-done((bf16[192,384]{1,0:T(8,128)(2,1)S(1)}, bf16[192,384]{1,0:T(8,128)(2,1)S(1)}, u32[]{:S(2)}, u32[]{:S(2)}) %collective-permute-start.49) | collective-permute-done | bytes 147488 | tf_op jit(solution)/shard_map/ppermute | solution.py:698
  209.5 2.5 %collective-permute-start.59 = (bf16[48,1920]{1,0:T(8,128)(2,1)S(1)}, bf16[48,1920]{1,0:T(8,128)(2,1)S(1)}, u32[]{:S(2)}, u32[]{:S(2)}) collective-permute-start(bf16[48,1920]{1,0:T(8,128)(2,1)S(1)} %get-tuple-element.211), channel_id=1, source_target_pairs={{0,6},{1,7},{2,0},{3,1},{4,2},{5,3},{6,4},{7,5},{8,14},{9,15},{10,... | collective-permute-start | bytes 552968 | tf_op jit(solution)/shard_map/ppermute | solution.py:704
  212.0 2.3 collective-permute-start.48
  218.5 4.0 %collective-permute-done.46.refs_4_ = bf16[2,48,1280]{2,1,0:T(8,128)(2,1)S(1)} collective-permute-done((bf16[2,48,1280]{2,1,0:T(8,128)(2,1)S(1)}, bf16[2,48,1280]{2,1,0:T(8,128)(2,1)S(1)}, u32[]{:S(2)}, u32[]{:S(2)}) %collective-permute-start.46) | collective-permute-done | bytes 245792 | tf_op jit(solution)/shard_map/ppermute | solution.py:701
  225.7 2.3 collective-permute-start.53
  228.0 2.4 collective-permute-start.60
  235.5 4.4 %collective-permute-start.54 = (bf16[48,1280]{1,0:T(8,128)(2,1)S(1)}, bf16[48,1280]{1,0:T(8,128)(2,1)S(1)}, u32[]{:S(2)}, u32[]{:S(2)}) collective-permute-start(bf16[48,1280]{1,0:T(8,128)(2,1)S(1)} %get-tuple-element.207.refs_1_), channel_id=1, source_target_pairs={{0,8},{8,0},{16,24},{24,16},{1,9},{9,1},{17,25},{25,17},{2,10},{10... | collective-permute-start | bytes 368648 | tf_op jit(solution)/shard_map/ppermute | solution.py:695
  239.9 3.3 %collective-permute-start.56 = (bf16[48,1280]{1,0:T(8,128)(2,1)S(1)}, bf16[48,1280]{1,0:T(8,128)(2,1)S(1)}, u32[]{:S(2)}, u32[]{:S(2)}) collective-permute-start(bf16[48,1280]{1,0:T(8,128)(2,1)S(1)} %collective-permute-done.55.refs_3_), channel_id=1, source_target_pairs={{0,8},{8,0},{16,24},{24,16},{1,9},{9,1},{17,25},{25,17},{2,10},{10... | collective-permute-start | bytes 368648 | tf_op jit(solution)/shard_map/ppermute | solution.py:695
  (188 shorter events, 74.2 us)
Async XLA Ops:
  7.6 10.4 %collective-permute-start.1 = (bf16[48,1280]{1,0:T(8,128)(2,1)S(1)}, bf16[48,1280]{1,0:T(8,128)(2,1)S(1)}, u32[]{:S(2)}, u32[]{:S(2)}) collective-permute-start(bf16[48,1280]{1,0:T(8,128)(2,1)S(1)} %get-tuple-element.122.refs_1_), channel_id=1, source_target_pairs={{0,4},{1,5},{2,6},{3,7},{4,0},{5,1},{6,2},{7,3},{8,12},{9,13},{10,... | collective-permute-start | bytes 368648 | tf_op jit(solution)/shard_map/ppermute | solution.py:704
  7.6 10.4 %collective-permute-start = (bf16[48,1280]{1,0:T(8,128)(2,1)S(1)}, bf16[48,1280]{1,0:T(8,128)(2,1)S(1)}, u32[]{:S(2)}, u32[]{:S(2)}) collective-permute-start(bf16[48,1280]{1,0:T(8,128)(2,1)S(1)} %get-tuple-element.122.refs_1_), channel_id=1, source_target_pairs={{0,2},{1,3},{2,4},{3,5},{4,6},{5,7},{6,0},{7,1},{8,10},{9,11},{10,... | collective-permute-start | bytes 368648 | tf_op jit(solution)/shard_map/ppermute | solution.py:704
  18.5 19.3 %collective-permute-start.4 = (bf16[48,5120]{1,0:T(8,128)(2,1)S(1)}, bf16[48,5120]{1,0:T(8,128)(2,1)S(1)}, u32[]{:S(2)}, u32[]{:S(2)}) collective-permute-start(bf16[48,5120]{1,0:T(8,128)(2,1)S(1)} %shard_map.290.refs_1_), channel_id=1, source_target_pairs={{0,16},{8,24},{16,0},{24,8},{1,17},{9,25},{17,1},{25,9},{2,18},{10... | collective-permute-start | bytes 1474568 | tf_op jit(solution)/shard_map/ppermute | solution.py:698
  19.8 18.0 %collective-permute-start.3 = (bf16[48,5120]{1,0:T(8,128)(2,1)S(1)}, bf16[48,5120]{1,0:T(8,128)(2,1)S(1)}, u32[]{:S(2)}, u32[]{:S(2)}) collective-permute-start(bf16[48,5120]{1,0:T(8,128)(2,1)S(1)} %shard_map.290.refs_1_), channel_id=1, source_target_pairs={{0,1},{1,0},{2,3},{3,2},{4,5},{5,4},{6,7},{7,6},{8,9},{9,8},{10,11... | collective-permute-start | bytes 1474568 | tf_op jit(solution)/shard_map/ppermute | solution.py:701
  21.4 16.5 %collective-permute-start.6 = (bf16[48,1920]{1,0:T(8,128)(2,1)S(1)}, bf16[48,1920]{1,0:T(8,128)(2,1)S(1)}, u32[]{:S(2)}, u32[]{:S(2)}) collective-permute-start(bf16[48,1920]{1,0:T(8,128)(2,1)S(1)} %get-tuple-element.123.refs_4_.refs_1_), channel_id=1, source_target_pairs={{0,4},{1,5},{2,6},{3,7},{4,0},{5,1},{6,2},{7,3},{8,12},{9,13},{10,... | collective-permute-start | bytes 552968 | tf_op jit(solution)/shard_map/ppermute | solution.py:704
  23.2 14.7 %collective-permute-start.5 = (bf16[48,1920]{1,0:T(8,128)(2,1)S(1)}, bf16[48,1920]{1,0:T(8,128)(2,1)S(1)}, u32[]{:S(2)}, u32[]{:S(2)}) collective-permute-start(bf16[48,1920]{1,0:T(8,128)(2,1)S(1)} %get-tuple-element.123.refs_4_.refs_1_), channel_id=1, source_target_pairs={{0,2},{1,3},{2,4},{3,5},{4,6},{5,7},{6,0},{7,1},{8,10},{9,11},{10,... | collective-permute-start | bytes 552968 | tf_op jit(solution)/shard_map/ppermute | solution.py:704
  38.5 16.2 %collective-permute-start.8 = (bf16[48,15360]{1,0:T(8,128)(2,1)S(1)}, bf16[48,15360]{1,0:T(8,128)(2,1)S(1)}, u32[]{:S(2)}, u32[]{:S(2)}) collective-permute-start(bf16[48,15360]{1,0:T(8,128)(2,1)S(1)} %get-tuple-element.124.refs_4_), channel_id=1, source_target_pairs={{0,8},{8,0},{16,24},{24,16},{1,9},{9,1},{17,25},{25,17},{2,10},{10... | collective-permute-start | bytes 4423688 | tf_op jit(solution)/shard_map/ppermute | solution.py:695
  49.5 20.0 %collective-permute-start.14 = (bf16[48,7680]{1,0:T(8,128)(2,1)S(1)}, bf16[48,7680]{1,0:T(8,128)(2,1)S(1)}, u32[]{:S(2)}, u32[]{:S(2)}) collective-permute-start(bf16[48,7680]{1,0:T(8,128)(2,1)S(1)} %shard_map.292.refs_10_.refs_1_), channel_id=1, source_target_pairs={{0,16},{8,24},{16,0},{24,8},{1,17},{9,25},{17,1},{25,9},{2,18},{10... | collective-permute-start | bytes 2211848 | tf_op jit(solution)/shard_map/ppermute | solution.py:698
  49.8 19.7 %collective-permute-start.13 = (bf16[48,7680]{1,0:T(8,128)(2,1)S(1)}, bf16[48,7680]{1,0:T(8,128)(2,1)S(1)}, u32[]{:S(2)}, u32[]{:S(2)}) collective-permute-start(bf16[48,7680]{1,0:T(8,128)(2,1)S(1)} %shard_map.292.refs_10_.refs_1_), channel_id=1, source_target_pairs={{0,1},{1,0},{2,3},{3,2},{4,5},{5,4},{6,7},{7,6},{8,9},{9,8},{10,11... | collective-permute-start | bytes 2211848 | tf_op jit(solution)/shard_map/ppermute | solution.py:701
  53.8 15.6 %collective-permute-start.17 = (bf16[48,1536]{1,0:T(8,128)(2,1)S(1)}, bf16[48,1536]{1,0:T(8,128)(2,1)S(1)}, u32[]{:S(2)}, u32[]{:S(2)}) collective-permute-start(bf16[48,1536]{1,0:T(8,128)(2,1)S(1)} %get-tuple-element.131.refs_5_.refs_1_), channel_id=1, source_target_pairs={{0,6},{1,7},{2,0},{3,1},{4,2},{5,3},{6,4},{7,5},{8,14},{9,15},{10,... | collective-permute-start | bytes 442376 | tf_op jit(solution)/shard_map/ppermute | solution.py:704
  54.2 15.2 %collective-permute-start.16 = (bf16[48,1536]{1,0:T(8,128)(2,1)S(1)}, bf16[48,1536]{1,0:T(8,128)(2,1)S(1)}, u32[]{:S(2)}, u32[]{:S(2)}) collective-permute-start(bf16[48,1536]{1,0:T(8,128)(2,1)S(1)} %get-tuple-element.131.refs_5_.refs_1_), channel_id=1, source_target_pairs={{0,4},{1,5},{2,6},{3,7},{4,0},{5,1},{6,2},{7,3},{8,12},{9,13},{10,... | collective-permute-start | bytes 442376 | tf_op jit(solution)/shard_map/ppermute | solution.py:704
  54.8 14.7 %collective-permute-start.15 = (bf16[48,1536]{1,0:T(8,128)(2,1)S(1)}, bf16[48,1536]{1,0:T(8,128)(2,1)S(1)}, u32[]{:S(2)}, u32[]{:S(2)}) collective-permute-start(bf16[48,1536]{1,0:T(8,128)(2,1)S(1)} %get-tuple-element.131.refs_5_.refs_1_), channel_id=1, source_target_pairs={{0,2},{1,3},{2,4},{3,5},{4,6},{5,7},{6,0},{7,1},{8,10},{9,11},{10,... | collective-permute-start | bytes 442376 | tf_op jit(solution)/shard_map/ppermute | solution.py:704
  70.3 15.6 %collective-permute-start.18 = (bf16[48,23040]{1,0:T(8,128)(2,1)S(1)}, bf16[48,23040]{1,0:T(8,128)(2,1)S(1)}, u32[]{:S(2)}, u32[]{:S(2)}) collective-permute-start(bf16[48,23040]{1,0:T(8,128)(2,1)S(1)} %get-tuple-element.132.refs_7_), channel_id=1, source_target_pairs={{0,8},{8,0},{16,24},{24,16},{1,9},{9,1},{17,25},{25,17},{2,10},{10... | collective-permute-start | bytes 6635528 | tf_op jit(solution)/shard_map/ppermute | solution.py:695
  72.8 10.2 %collective-permute-start.19 = (bf16[48,3840]{1,0:T(8,128)(2,1)S(1)}, bf16[48,3840]{1,0:T(8,128)(2,1)S(1)}, u32[]{:S(2)}, u32[]{:S(2)}) collective-permute-start(bf16[48,3840]{1,0:T(8,128)(2,1)S(1)} %get-tuple-element.133.refs_5_), channel_id=1, source_target_pairs={{0,1},{1,0},{2,3},{3,2},{4,5},{5,4},{6,7},{7,6},{8,9},{9,8},{10,11... | collective-permute-start | bytes 1105928 | tf_op jit(solution)/shard_map/ppermute | solution.py:701
  73.6 22.4 %collective-permute-start.24 = (bf16[48,6144]{1,0:T(8,128)(2,1)S(1)}, bf16[48,6144]{1,0:T(8,128)(2,1)S(1)}, u32[]{:S(2)}, u32[]{:S(2)}) collective-permute-start(bf16[48,6144]{1,0:T(8,128)(2,1)S(1)} %shard_map.296.refs_13_.refs_1_), channel_id=1, source_target_pairs={{0,16},{8,24},{16,0},{24,8},{1,17},{9,25},{17,1},{25,9},{2,18},{10... | collective-permute-start | bytes 1769480 | tf_op jit(solution)/shard_map/ppermute | solution.py:698
  73.9 22.1 %collective-permute-start.23 = (bf16[48,6144]{1,0:T(8,128)(2,1)S(1)}, bf16[48,6144]{1,0:T(8,128)(2,1)S(1)}, u32[]{:S(2)}, u32[]{:S(2)}) collective-permute-start(bf16[48,6144]{1,0:T(8,128)(2,1)S(1)} %shard_map.296.refs_13_.refs_1_), channel_id=1, source_target_pairs={{0,1},{1,0},{2,3},{3,2},{4,5},{5,4},{6,7},{7,6},{8,9},{9,8},{10,11... | collective-permute-start | bytes 1769480 | tf_op jit(solution)/shard_map/ppermute | solution.py:701
  96.8 13.8 %collective-permute-start.25 = (bf16[48,18432]{1,0:T(8,128)(2,1)S(1)}, bf16[48,18432]{1,0:T(8,128)(2,1)S(1)}, u32[]{:S(2)}, u32[]{:S(2)}) collective-permute-start(bf16[48,18432]{1,0:T(8,128)(2,1)S(1)} %get-tuple-element.143.refs_8_), channel_id=1, source_target_pairs={{0,8},{8,0},{16,24},{24,16},{1,9},{9,1},{17,25},{25,17},{2,10},{10... | collective-permute-start | bytes 5308424 | tf_op jit(solution)/shard_map/ppermute | solution.py:695
  142.0 22.2 %collective-permute-start.32 = (bf16[4,192,384]{2,1,0:T(8,128)(2,1)S(1)}, bf16[4,192,384]{2,1,0:T(8,128)(2,1)S(1)}, u32[]{:S(2)}, u32[]{:S(2)}) collective-permute-start(bf16[4,192,384]{2,1,0:T(8,128)(2,1)S(1)} %get-tuple-element.164), channel_id=1, source_target_pairs={{0,1},{1,0},{2,3},{3,2},{4,5},{5,4},{6,7},{7,6},{8,9},{9,8},{10,11... | collective-permute-start | bytes 1769480 | tf_op jit(solution)/shard_map/ppermute | solution.py:701
  142.3 21.9 %collective-permute-start.33 = (bf16[4,192,384]{2,1,0:T(8,128)(2,1)S(1)}, bf16[4,192,384]{2,1,0:T(8,128)(2,1)S(1)}, u32[]{:S(2)}, u32[]{:S(2)}) collective-permute-start(bf16[4,192,384]{2,1,0:T(8,128)(2,1)S(1)} %get-tuple-element.165), channel_id=1, source_target_pairs={{0,16},{8,24},{16,0},{24,8},{1,17},{9,25},{17,1},{25,9},{2,18},{10... | collective-permute-start | bytes 1769480 | tf_op jit(solution)/shard_map/ppermute | solution.py:698
  154.9 17.5 %collective-permute-start.34 = (bf16[4,48,1920]{2,1,0:T(8,128)(2,1)S(1)}, bf16[4,48,1920]{2,1,0:T(8,128)(2,1)S(1)}, u32[]{:S(2)}, u32[]{:S(2)}) collective-permute-start(bf16[4,48,1920]{2,1,0:T(8,128)(2,1)S(1)} %get-tuple-element.172), channel_id=1, source_target_pairs={{0,1},{1,0},{2,3},{3,2},{4,5},{5,4},{6,7},{7,6},{8,9},{9,8},{10,11... | collective-permute-start | bytes 2211848 | tf_op jit(solution)/shard_map/ppermute | solution.py:701
  156.2 17.1 %collective-permute-start.35 = (bf16[4,48,1920]{2,1,0:T(8,128)(2,1)S(1)}, bf16[4,48,1920]{2,1,0:T(8,128)(2,1)S(1)}, u32[]{:S(2)}, u32[]{:S(2)}) collective-permute-start(bf16[4,48,1920]{2,1,0:T(8,128)(2,1)S(1)} %get-tuple-element.173), channel_id=1, source_target_pairs={{0,16},{8,24},{16,0},{24,8},{1,17},{9,25},{17,1},{25,9},{2,18},{10... | collective-permute-start | bytes 2211848 | tf_op jit(solution)/shard_map/ppermute | solution.py:698
  179.4 15.3 %collective-permute-start.44 = (bf16[2,48,1920]{2,1,0:T(8,128)(2,1)S(1)}, bf16[2,48,1920]{2,1,0:T(8,128)(2,1)S(1)}, u32[]{:S(2)}, u32[]{:S(2)}) collective-permute-start(bf16[2,48,1920]{2,1,0:T(8,128)(2,1)S(1)} %get-tuple-element.193), channel_id=1, source_target_pairs={{0,1},{1,0},{2,3},{3,2},{4,5},{5,4},{6,7},{7,6},{8,9},{9,8},{10,11... | collective-permute-start | bytes 1105928 | tf_op jit(solution)/shard_map/ppermute | solution.py:701
  179.9 15.1 %collective-permute-start.45 = (bf16[2,48,1920]{2,1,0:T(8,128)(2,1)S(1)}, bf16[2,48,1920]{2,1,0:T(8,128)(2,1)S(1)}, u32[]{:S(2)}, u32[]{:S(2)}) collective-permute-start(bf16[2,48,1920]{2,1,0:T(8,128)(2,1)S(1)} %get-tuple-element.194), channel_id=1, source_target_pairs={{0,16},{8,24},{16,0},{24,8},{1,17},{9,25},{17,1},{25,9},{2,18},{10... | collective-permute-start | bytes 1105928 | tf_op jit(solution)/shard_map/ppermute | solution.py:698
  188.6 12.9 %collective-permute-start.42 = (bf16[192,384]{1,0:T(8,128)(2,1)S(1)}, bf16[192,384]{1,0:T(8,128)(2,1)S(1)}, u32[]{:S(2)}, u32[]{:S(2)}) collective-permute-start(bf16[192,384]{1,0:T(8,128)(2,1)S(1)} %get-tuple-element.190), channel_id=1, source_target_pairs={{0,4},{1,5},{2,6},{3,7},{4,0},{5,1},{6,2},{7,3},{8,12},{9,13},{10,... | collective-permute-start | bytes 442376 | tf_op jit(solution)/shard_map/ppermute | solution.py:704
  190.4 11.1 %collective-permute-start.43 = (bf16[192,384]{1,0:T(8,128)(2,1)S(1)}, bf16[192,384]{1,0:T(8,128)(2,1)S(1)}, u32[]{:S(2)}, u32[]{:S(2)}) collective-permute-start(bf16[192,384]{1,0:T(8,128)(2,1)S(1)} %get-tuple-element.191), channel_id=1, source_target_pairs={{0,6},{1,7},{2,0},{3,1},{4,2},{5,3},{6,4},{7,5},{8,14},{9,15},{10,... | collective-permute-start | bytes 442376 | tf_op jit(solution)/shard_map/ppermute | solution.py:704
  194.7 17.3 %collective-permute-start.37 = (bf16[4,48,1280]{2,1,0:T(8,128)(2,1)S(1)}, bf16[4,48,1280]{2,1,0:T(8,128)(2,1)S(1)}, u32[]{:S(2)}, u32[]{:S(2)}) collective-permute-start(bf16[4,48,1280]{2,1,0:T(8,128)(2,1)S(1)} %get-tuple-element.180), channel_id=1, source_target_pairs={{0,1},{1,0},{2,3},{3,2},{4,5},{5,4},{6,7},{7,6},{8,9},{9,8},{10,11... | collective-permute-start | bytes 1474568 | tf_op jit(solution)/shard_map/ppermute | solution.py:701
  194.9 19.4 %collective-permute-start.38 = (bf16[4,48,1280]{2,1,0:T(8,128)(2,1)S(1)}, bf16[4,48,1280]{2,1,0:T(8,128)(2,1)S(1)}, u32[]{:S(2)}, u32[]{:S(2)}) collective-permute-start(bf16[4,48,1280]{2,1,0:T(8,128)(2,1)S(1)} %get-tuple-element.181), channel_id=1, source_target_pairs={{0,16},{8,24},{16,0},{24,8},{1,17},{9,25},{17,1},{25,9},{2,18},{10... | collective-permute-start | bytes 1474568 | tf_op jit(solution)/shard_map/ppermute | solution.py:698
  202.5 21.8 %collective-permute-start.57 = (bf16[48,1920]{1,0:T(8,128)(2,1)S(1)}, bf16[48,1920]{1,0:T(8,128)(2,1)S(1)}, u32[]{:S(2)}, u32[]{:S(2)}) collective-permute-start(bf16[48,1920]{1,0:T(8,128)(2,1)S(1)} %get-tuple-element.209), channel_id=1, source_target_pairs={{0,2},{1,3},{2,4},{3,5},{4,6},{5,7},{6,0},{7,1},{8,10},{9,11},{10,... | collective-permute-start | bytes 552968 | tf_op jit(solution)/shard_map/ppermute | solution.py:704
  206.0 18.4 %collective-permute-start.58 = (bf16[48,1920]{1,0:T(8,128)(2,1)S(1)}, bf16[48,1920]{1,0:T(8,128)(2,1)S(1)}, u32[]{:S(2)}, u32[]{:S(2)}) collective-permute-start(bf16[48,1920]{1,0:T(8,128)(2,1)S(1)} %get-tuple-element.210), channel_id=1, source_target_pairs={{0,4},{1,5},{2,6},{3,7},{4,0},{5,1},{6,2},{7,3},{8,12},{9,13},{10,... | collective-permute-start | bytes 552968 | tf_op jit(solution)/shard_map/ppermute | solution.py:704
  209.5 14.8 %collective-permute-start.59 = (bf16[48,1920]{1,0:T(8,128)(2,1)S(1)}, bf16[48,1920]{1,0:T(8,128)(2,1)S(1)}, u32[]{:S(2)}, u32[]{:S(2)}) collective-permute-start(bf16[48,1920]{1,0:T(8,128)(2,1)S(1)} %get-tuple-element.211), channel_id=1, source_target_pairs={{0,6},{1,7},{2,0},{3,1},{4,2},{5,3},{6,4},{7,5},{8,14},{9,15},{10,... | collective-permute-start | bytes 552968 | tf_op jit(solution)/shard_map/ppermute | solution.py:704
  228.0 15.2 %collective-permute-start.60 = (bf16[48,1920]{1,0:T(8,128)(2,1)S(1)}, bf16[48,1920]{1,0:T(8,128)(2,1)S(1)}, u32[]{:S(2)}, u32[]{:S(2)}) collective-permute-start(bf16[48,1920]{1,0:T(8,128)(2,1)S(1)} %get-tuple-element.213.refs_1_), channel_id=1, source_target_pairs={{0,8},{8,0},{16,24},{24,16},{1,9},{9,1},{17,25},{25,17},{2,10},{10... | collective-permute-start | bytes 552968 | tf_op jit(solution)/shard_map/ppermute | solution.py:695
  230.4 12.9 %collective-permute-start.62 = (bf16[48,1920]{1,0:T(8,128)(2,1)S(1)}, bf16[48,1920]{1,0:T(8,128)(2,1)S(1)}, u32[]{:S(2)}, u32[]{:S(2)}) collective-permute-start(bf16[48,1920]{1,0:T(8,128)(2,1)S(1)} %collective-permute-done.61.refs_3_), channel_id=1, source_target_pairs={{0,8},{8,0},{16,24},{24,16},{1,9},{9,1},{17,25},{25,17},{2,10},{10... | collective-permute-start | bytes 552968 | tf_op jit(solution)/shard_map/ppermute | solution.py:695
  (59 other events, 448.5 us)
